TPU v7x, 512 devices: a whole 4x8x8 slice. The times are simulated.
512 devices in a mesh: dp: 8 (over z_lo, x), dap: 64 (over z_hi, y, core).
Axes of the slice: x: 4, y: 8, z: 8 (z_hi: 4, z_lo: 2; z = z_hi * 2 + z_lo), core: 2. Of those that a mesh axis runs over, the one named last changes fastest.
Arguments:
- pair_act: bfloat16 [2048, 256, 128], P(('dp', 'dap')), parts along dimension 0, may hold values from -6 to 6
- cotangent: bfloat16 [2048, 256, 128], P(('dp', 'dap')), parts along dimension 0, may hold values from -16 to 16
- bias_start: bfloat16 [2048, 4, 256], P('dp'), parts along dimension 0, may hold values from -4 to 352
- bias_end: bfloat16 [2048, 4, 256], P('dp'), parts along dimension 0, may hold values from -4 to 352
- w_in_start: bfloat16 [128, 512], replicated, may hold values from -0.5 to 0.5
- w_out_start: bfloat16 [128, 128], replicated, may hold values from -0.5 to 0.5
- w_in_end: bfloat16 [128, 512], replicated, may hold values from -0.5 to 0.5
- w_out_end: bfloat16 [128, 128], replicated, may hold values from -0.5 to 0.5
- residue_mask: int32 [32768], P('dp'), parts along dimension 0, may hold values 0 or 1
- window_offset: int32 [8], P('dp'), parts along dimension 0, may hold values from 0 to 3840
Outputs:
- grad_pair: bfloat16 [2048, 256, 128], P(('dp', 'dap')), parts along dimension 0
- grad_bias_start: float32 [2048, 4, 256], P(('dp', 'dap')), parts along dimension 0
- grad_bias_end: float32 [2048, 4, 256], P(('dp', 'dap')), parts along dimension 0
- grad_in_start: float32 [1024, 512], P('dp'), parts along dimension 0
- grad_out_start: float32 [1024, 128], P('dp'), parts along dimension 0
- grad_in_end: float32 [1024, 512], P('dp'), parts along dimension 0
- grad_out_end: float32 [1024, 128], P('dp'), parts along dimension 0
There are 8 independent parts, one for each index of `dp`. A program takes and returns all parts, laid end to end along the dimension named above; an argument that names none is the same for every part. Nothing has to cross between parts.
All inputs are finite; a program needn't handle non-finite values.
Results may differ from a plain program's by a relative error of at most 0.015.
Values may be sent and summed in bfloat16 or wider, within the bound.
No kernel may reach another device: no remote copies, remote signals or barrier semaphores. Data moves between devices by JAX's collectives and lax.ppermute only.
A program may use at most 64 MiB of HBM per device.

v0:
```python
import jax
import jax.numpy as jnp
from jax import lax
from jax.sharding import PartitionSpec as P

H = 4
DH = 32


ln_epsilon = 1e-05
mask_penalty = 1000000000.0


def product(formula, first_operand, second_operand):
    return jnp.einsum(formula, first_operand, second_operand, preferred_element_type=jnp.float32)


def layer_stats(activations):
    values = activations.astype(jnp.float32)
    centred = values - jnp.mean(values, axis=-1, keepdims=True)
    inv_std = lax.rsqrt(jnp.mean(centred * centred, axis=-1, keepdims=True) + ln_epsilon)
    return (centred * inv_std, inv_std)


def softmax_rows(queries, key_rows, pair_bias, penalty):
    scores = (
        product("rjhd,rkhd->rjhk", queries, key_rows)
        + pair_bias.astype(jnp.float32)[None]
        + penalty
    )
    row_peak = jnp.max(scores, axis=-1, keepdims=True)
    exponent = jnp.exp(scores - row_peak)
    return exponent / jnp.sum(exponent, axis=-1, keepdims=True)


def attention_forward(activations, pair_bias, penalty, w_in, w_out):
    row_count, length = (activations.shape[0], activations.shape[1])
    hidden = w_out.shape[0]
    normed_f32, inv_std = layer_stats(activations)
    normed = normed_f32.astype(jnp.bfloat16)
    projected = product("rjc,cf->rjf", normed, w_in)
    queries = (
        (projected[..., :hidden] * DH ** (-0.5))
        .astype(jnp.bfloat16)
        .reshape(row_count, length, H, DH)
    )
    key_rows = (
        projected[..., hidden : 2 * hidden].astype(jnp.bfloat16).reshape(row_count, length, H, DH)
    )
    value_rows = (
        projected[..., 2 * hidden : 3 * hidden]
        .astype(jnp.bfloat16)
        .reshape(row_count, length, H, DH)
    )
    gate_value = jax.nn.sigmoid(projected[..., 3 * hidden :])
    probs_f32 = softmax_rows(queries, key_rows, pair_bias, penalty)
    probs_b16 = probs_f32.astype(jnp.bfloat16)
    attended = product("rjhk,rkhd->rjhd", probs_b16, value_rows).reshape(row_count, length, hidden)
    gated_out = (gate_value * attended).astype(jnp.bfloat16)
    output = (activations.astype(jnp.float32) + product("rjf,fc->rjc", gated_out, w_out)).astype(
        jnp.bfloat16
    )
    return (
        output,
        (
            normed_f32,
            inv_std,
            normed,
            queries,
            key_rows,
            value_rows,
            gate_value,
            attended,
            gated_out,
            probs_f32,
            probs_b16,
        ),
    )


def attention_backward(state_tuple, upstream, w_in, w_out):
    (
        normed_f32,
        inv_std,
        normed,
        queries,
        key_rows,
        value_rows,
        gate_value,
        attended,
        gated_out,
        probs_f32,
        probs_b16,
    ) = state_tuple
    row_count, length = (upstream.shape[0], upstream.shape[1])
    hidden = w_out.shape[0]
    grad_wout = product("rjf,rjc->fc", gated_out, upstream)
    grad_gated = product("rjc,fc->rjf", upstream, w_out)
    grad_gate = grad_gated * attended * gate_value * (1.0 - gate_value)
    grad_mixed = (grad_gated * gate_value).astype(jnp.bfloat16).reshape(row_count, length, H, DH)
    grad_probs = product("rjhd,rkhd->rjhk", grad_mixed, value_rows)
    grad_value = product("rjhk,rjhd->rkhd", probs_b16, grad_mixed)
    grad_scores = probs_f32 * (grad_probs - jnp.sum(probs_f32 * grad_probs, axis=-1, keepdims=True))
    scores_b16 = grad_scores.astype(jnp.bfloat16)
    grad_query = product("rjhk,rkhd->rjhd", scores_b16, key_rows) * DH ** (-0.5)
    grad_key = product("rjhk,rjhd->rkhd", scores_b16, queries)
    grad_proj = jnp.concatenate(
        [
            grad_query.reshape(row_count, length, hidden),
            grad_key.reshape(row_count, length, hidden),
            grad_value.reshape(row_count, length, hidden),
            grad_gate,
        ],
        axis=-1,
    ).astype(jnp.bfloat16)
    grad_win = product("rjc,rjf->cf", normed, grad_proj)
    grad_normed = product("rjf,cf->rjc", grad_proj, w_in)
    centred_grad = (
        grad_normed
        - jnp.mean(grad_normed, axis=-1, keepdims=True)
        - normed_f32 * jnp.mean(grad_normed * normed_f32, axis=-1, keepdims=True)
    )
    grad_block = upstream.astype(jnp.float32) + inv_std * centred_grad
    return (grad_block, grad_scores, grad_win, grad_wout, grad_mixed)


def backward_and_reduce(state_tuple, upstream, w_in, w_out):
    grad_block, grad_scores, grad_win, grad_wout, grad_mixed = attention_backward(
        state_tuple, upstream, w_in, w_out
    )
    grad_bias = lax.psum_scatter(
        jnp.sum(grad_scores, axis=0), "dap", scatter_dimension=0, tiled=True
    )
    return (grad_block, grad_bias, grad_win, grad_wout)


def shards(
    pair_act,
    cotangent,
    bias_start,
    bias_end,
    w_in_start,
    w_out_start,
    w_in_end,
    w_out_end,
    residue_mask,
    window_offset,
):
    length = pair_act.shape[1]
    window = lax.dynamic_slice_in_dim(residue_mask, window_offset[0], length)
    penalty = (window.astype(jnp.float32) - 1.0) * mask_penalty
    first_out, start_state = attention_forward(
        pair_act, bias_start, penalty, w_in_start, w_out_start
    )
    first_cols, cotangent_cols = (
        lax.all_to_all(first_out, "dap", split_axis=1, concat_axis=0, tiled=True),
        lax.all_to_all(cotangent, "dap", split_axis=1, concat_axis=0, tiled=True),
    )
    columns = jnp.swapaxes(first_cols, 0, 1)
    upstream = jnp.swapaxes(cotangent_cols, 0, 1)
    end_state = attention_forward(columns, bias_end, penalty, w_in_end, w_out_end)[1]
    grad_cols, grad_bias_end, in_end, out_end = backward_and_reduce(
        end_state, upstream, w_in_end, w_out_end
    )
    grad_back = lax.all_to_all(
        grad_cols.astype(jnp.bfloat16), "dap", split_axis=1, concat_axis=0, tiled=True
    )
    grad_first = jnp.swapaxes(grad_back, 0, 1)
    grad_rows, grad_bias_start, in_start, out_start = backward_and_reduce(
        start_state, grad_first, w_in_start, w_out_start
    )
    weight_grads = lax.psum((in_start, out_start, in_end, out_end), "dap")
    return (
        grad_rows.astype(jnp.bfloat16),
        grad_bias_start,
        grad_bias_end,
        weight_grads[0] / length,
        weight_grads[1] / length,
        weight_grads[2] / length,
        weight_grads[3] / length,
    )


def solution(mesh):
    placed = (
        P(("dp", "dap"), None, None),
        P(("dp", "dap"), None, None),
        P("dp", None, None),
        P("dp", None, None),
        P(),
        P(),
        P(),
        P(),
        P("dp"),
        P("dp"),
    )
    return jax.shard_map(
        shards,
        mesh=mesh,
        in_specs=placed,
        out_specs=(
            P(("dp", "dap"), None, None),
            P(("dp", "dap"), None, None),
            P(("dp", "dap"), None, None),
            P("dp", None),
            P("dp", None),
            P("dp", None),
            P("dp", None),
        ),
        check_vma=False,
    )
```

profile of v0, /device:TPU:1, one launch (start us, length us, event | category | flops | bytes accessed | tf_op | source)
XLA Modules:
  0.0 722.1 jit_solution(8386406448534142082)
XLA Ops:
  7.2 1.9 copy.109
  9.1 17.6 %all-to-all-start = ((bf16[4,256,128]{2,0,1:T(4,128)(2,1)}), bf16[4,256,128]{2,0,1:T(4,128)(2,1)S(1)}, u32[]{:S(2)}, u32[]{:S(2)}) async-start(bf16[4,256,128]{2,0,1:T(4,128)(2,1)} %copy.109), calls=%async_computation | async-start | bytes 524288 | tf_op jit(solution)/shard_map/all_to_all | solution.py:157
  29.9 2.4 copy.114
  35.0 5.3 fusion.82
  40.3 3.5 fusion.31
  47.8 12.7 %all-to-all-start.1 = ((bf16[4,256,128]{2,0,1:T(4,128)(2,1)}), bf16[4,256,128]{2,0,1:T(4,128)(2,1)S(1)}, u32[]{:S(2)}, u32[]{:S(2)}) async-start(bf16[4,256,128]{2,0,1:T(4,128)(2,1)} %copy.117), calls=%async_computation.1 | async-start | bytes 524288 | tf_op jit(solution)/shard_map/all_to_all | solution.py:156
  60.5 2.4 copy.121
  64.0 10.4 %all-to-all-done.1 = bf16[4,256,128]{2,0,1:T(4,128)(2,1)S(1)} async-done(((bf16[4,256,128]{2,0,1:T(4,128)(2,1)}), bf16[4,256,128]{2,0,1:T(4,128)(2,1)S(1)}, u32[]{:S(2)}, u32[]{:S(2)}) %all-to-all-start.1) | async-done | bytes 262176 | tf_op jit(solution)/shard_map/all_to_all | solution.py:156
  75.1 1.9 fusion.83
  84.3 5.4 fusion.84
  89.7 3.5 fusion.27
  93.2 2.1 copy.130
  95.3 2.4 multiply_convert_fusion.4
  99.4 3.8 convolution_convert_fusion.2
  104.1 2.1 fusion.20
  109.9 1.9 copy.131
  112.6 3.0 fusion.85
  120.5 6.6 all-to-all-start.2
  127.4 2.5 copy.151
  129.9 2.2 convolution_bitcast_fusion.2
  133.7 7.2 all-to-all-done.2
  141.9 1.9 multiply_convert_fusion.2
  145.9 3.1 convolution_convert_fusion
  160.5 545.7 %all-reduce.5.cloned.1.call-done = (f32[256,4,256]{2,1,0:T(4,128)}, f32[256,4,256]{2,1,0:T(4,128)}, f32[128,512]{1,0:T(8,128)}, f32[128,128]{1,0:T(8,128)}, f32[128,512]{1,0:T(8,128)}, /*index=5*/f32[128,128]{1,0:T(8,128)}) async-done(((f32[256,4,256]{2,1,0:T(4,128)}, f32[256,4,256]{2,1,0:T(4,128)}, f32[128,512]{1,0:T(8,128)}, f32[128,128]{1,0:T(8,128)}, f32[128,512]{1,0:T(8,128)}, ...) | async-done | bytes 2752528
  (132 shorter events, 54.8 us)
Async XLA Ops:
  7.2 67.9 %copy-start = (bf16[128,512]{1,0:T(8,128)(2,1)S(1)}, bf16[128,512]{1,0:T(8,128)(2,1)}, u32[]{:S(2)}) copy-start(bf16[128,512]{1,0:T(8,128)(2,1)} %param.16) | copy-start | bytes 393220
  7.2 25.1 %copy-start.1 = (bf16[4,256,128]{2,1,0:T(8,128)(2,1)S(1)}, bf16[4,256,128]{2,1,0:T(8,128)(2,1)}, u32[]{:S(2)}) copy-start(bf16[4,256,128]{2,1,0:T(8,128)(2,1)} %param.10) | copy-start | bytes 786436
  7.2 25.1 %copy-start.25 = (bf16[128,512]{1,0:T(8,128)(2,1)S(1)}, bf16[128,512]{1,0:T(8,128)(2,1)}, u32[]{:S(2)}) copy-start(bf16[128,512]{1,0:T(8,128)(2,1)} %param.14) | copy-start | bytes 393220
  9.1 38.0 %all-to-all-start = ((bf16[4,256,128]{2,0,1:T(4,128)(2,1)}), bf16[4,256,128]{2,0,1:T(4,128)(2,1)S(1)}, u32[]{:S(2)}, u32[]{:S(2)}) async-start(bf16[4,256,128]{2,0,1:T(4,128)(2,1)} %copy.109), calls=%async_computation | async-start | bytes 524288 | tf_op jit(solution)/shard_map/all_to_all | solution.py:157
  33.0 7.3 %copy-start.8 = (bf16[4,256,128]{1,2,0:T(8,128)(2,1)}, bf16[4,256,128]{1,2,0:T(8,128)(2,1)S(1)}, u32[]{:S(2)}) copy-start(bf16[4,256,128]{1,2,0:T(8,128)(2,1)S(1)} %copy.112) | copy-start | bytes 786436
  34.1 6.2 copy-start.10
  35.0 5.4 copy-start.30
  35.0 5.4 copy-start.17
  45.0 17.9 %copy-start.6 = (f32[4,256,128]{2,1,0:T(8,128)}, f32[4,256,128]{2,1,0:T(8,128)S(1)}, u32[]{:S(2)}) copy-start(f32[4,256,128]{2,1,0:T(8,128)S(1)} %copy.116) | copy-start | bytes 1572868
  47.8 26.6 %all-to-all-start.1 = ((bf16[4,256,128]{2,0,1:T(4,128)(2,1)}), bf16[4,256,128]{2,0,1:T(4,128)(2,1)S(1)}, u32[]{:S(2)}, u32[]{:S(2)}) async-start(bf16[4,256,128]{2,0,1:T(4,128)(2,1)} %copy.117), calls=%async_computation.1 | async-start | bytes 524288 | tf_op jit(solution)/shard_map/all_to_all | solution.py:156
  64.0 31.2 %copy-start.12 = (bf16[4,64,4,128]{3,0,1,2:T(4,128)(2,1)}, bf16[4,64,4,128]{3,0,1,2:T(4,128)(2,1)S(1)}, u32[]{:S(2)}) copy-start(bf16[4,64,4,128]{3,0,1,2:T(4,128)(2,1)S(1)} %copy.110) | copy-start | bytes 786436
  99.4 3.8 copy-start.3
  99.4 3.8 copy-start.23
  99.4 3.8 copy-start.24
  99.4 3.8 copy-start.29
  107.6 4.2 copy-start.15
  109.9 5.7 copy-start.19
  119.6 10.3 %copy-start.13 = (bf16[4,64,4,128]{3,0,1,2:T(4,128)(2,1)S(1)}, bf16[4,64,4,128]{3,0,1,2:T(4,128)(2,1)}, u32[]{:S(2)}) copy-start(bf16[4,64,4,128]{3,0,1,2:T(4,128)(2,1)} %copy-done.12) | copy-start | bytes 786436
  120.5 20.4 %all-to-all-start.2 = ((bf16[4,256,128]{2,0,1:T(4,128)(2,1)}), bf16[4,256,128]{2,0,1:T(4,128)(2,1)}, u32[]{:S(2)}, u32[]{:S(2)}) async-start(bf16[4,256,128]{2,0,1:T(4,128)(2,1)} %copy.136), calls=%async_computation.2 | async-start | bytes 524288 | tf_op jit(solution)/shard_map/all_to_all | solution.py:165
  127.1 579.2 %all-reduce.5.cloned.1.call-start = ((), (), s32[]{:S(2)}) async-start(), calls=%async_computation.3 | async-start | bytes 5505024
  132.2 9.7 %copy-start.7 = (f32[4,256,128]{2,1,0:T(8,128)S(1)}, f32[4,256,128]{2,1,0:T(8,128)}, u32[]{:S(2)}) copy-start(f32[4,256,128]{2,1,0:T(8,128)} %copy-done.6) | copy-start | bytes 1572868
  133.7 10.2 %copy-start.5 = (bf16[4,256,128]{2,1,0:T(8,128)(2,1)S(1)}, bf16[4,256,128]{2,1,0:T(8,128)(2,1)}, u32[]{:S(2)}) copy-start(bf16[4,256,128]{2,1,0:T(8,128)(2,1)} %copy-done.4) | copy-start | bytes 786436
  145.8 3.5 copy-start.18
  145.8 3.5 copy-start.28
  (13 other events, 24.2 us)
Sparse Core Ops, SparseCore 0:
  156.1 550.0 all-reduce.4
where the time goes:
time: 725 us; the launch traced here: 722 us
  waiting for transfers between devices  563 us (78%)
  matrix products  46.3 us (6%)
  local copies, waits for them, and re-layouts  39.5 us (5%)
  starting transfers between devices  37.2 us (5%)
  other arithmetic  19.9 us (3%)
  between operations  15.8 us (2%)
    unnamed x2, waiting for transfers between devices  546 us
    dot_general x21, matrix products, product(): jnp.einsum(formula, first_operand, second_operand, preferred_element_type...  35.6 us
    all_to_all x1, starting transfers between devices, shards(): lax.all_to_all(cotangent, 'dap', split_axis=1, concat_axis=0, tiled=True)  17.6 us
  transfers between devices with their start and end apart: 4, of which 3 were waited for; matrix products, arithmetic and copies ran while one was open for 4% of the time, Pallas kernels for 0%

commit v1 on v0

v1 whole, which is shorter than its diff:
```python
import functools

import jax
import jax.numpy as jnp
from jax import lax
from jax.experimental import pallas as pl
from jax.experimental.pallas import tpu as pltpu
from jax.sharding import PartitionSpec as P

H = 4
DH = 32
N = 256
C = 128
R = 4
PEERS = N // R

LN_EPSILON = 1e-05
MASK_PENALTY = 1000000000.0

f32 = jnp.float32
bf16 = jnp.bfloat16

VMEM_LIMIT = 48 * 1024 * 1024


def dot(a, b, dims):
    return lax.dot_general(a, b, (dims, ((), ())), preferred_element_type=f32)


def nn(a, b):
    return dot(a, b, ((1,), (0,)))


def nt(a, b):
    return dot(a, b, ((1,), (1,)))


def head_masks():
    lane = lax.broadcasted_iota(jnp.int32, (N, C), 1) // DH
    return [lane == h for h in range(H)]


def masked(value, masks):
    zero = jnp.zeros_like(value)
    return [jnp.where(m, value, zero) for m in masks]


def layer_stats(values):
    centred = values - jnp.mean(values, axis=-1, keepdims=True)
    inv_std = lax.rsqrt(jnp.mean(centred * centred, axis=-1, keepdims=True) + LN_EPSILON)
    return centred * inv_std, inv_std


def project(normed, w_in):
    projected = nn(normed, w_in)
    queries = (projected[:, :C] * DH ** (-0.5)).astype(bf16)
    keys = projected[:, C : 2 * C].astype(bf16)
    values = projected[:, 2 * C : 3 * C].astype(bf16)
    gate = 1.0 / (1.0 + jnp.exp(-projected[:, 3 * C :]))
    return queries, keys, values, gate


def head_probs(key_h, queries, bias_h, penalty):
    scores = nt(key_h, queries) + bias_h.astype(f32) + penalty
    exponent = jnp.exp(scores - jnp.max(scores, axis=0, keepdims=True))
    return exponent * (1.0 / jnp.sum(exponent, axis=0, keepdims=True))


def pack_rows(value, r, stage, packed):
    stage[...] = value
    for residue in range(R):
        packed[pl.ds(r * R + residue, PEERS, stride=R * R), :] = stage[pl.ds(residue, PEERS, stride=R), :]


def start_forward_kernel(x_ref, cot_ref, bias_ref, pen_ref, w_in_ref, w_out_ref, send_ref, stage, first_packed, cot_packed):
    masks = head_masks()
    penalty = jnp.broadcast_to(pen_ref[...], (N, N))
    for r in range(R):
        x = x_ref[r].astype(f32)
        normed, _ = layer_stats(x)
        queries, keys, values, gate = project(normed.astype(bf16), w_in_ref[...])
        keys_h = masked(keys, masks)
        values_t = values.astype(f32).T.astype(bf16)
        attended_t = []
        for h in range(H):
            probs = head_probs(keys_h[h], queries, bias_ref[h], penalty)
            attended_t.append(nn(values_t[h * DH : (h + 1) * DH], probs.astype(bf16)))
        attended = jnp.concatenate(attended_t, axis=0).T
        gated = (gate * attended).astype(bf16)
        out = (x + nn(gated, w_out_ref[...])).astype(bf16).astype(f32)
        pack_rows(out, r, stage, first_packed)
        pack_rows(cot_ref[r].astype(f32), r, stage, cot_packed)
    send_ref[:, : R * R, :] = first_packed[...].reshape(PEERS, R * R, C).astype(bf16)
    send_ref[:, R * R :, :] = cot_packed[...].reshape(PEERS, R * R, C).astype(bf16)


def node_backward(
    r, x, upstream, bias_ref, penalty, w_in_ref, w_in_t_ref, w_out_ref, w_out_t_ref, masks, bias_sum, weight_sum
):
    normed, inv_std = layer_stats(x)
    normed_b = normed.astype(bf16)
    queries, keys, values, gate = project(normed_b, w_in_ref[...])
    keys_h = masked(keys, masks)
    values_h = masked(values, masks)
    values_t = values.astype(f32).T.astype(bf16)
    keys_t = keys.astype(f32).T.astype(bf16)
    probs = [head_probs(keys_h[h], queries, bias_ref[h], penalty) for h in range(H)]
    probs_b = [p.astype(bf16) for p in probs]
    attended = jnp.concatenate([nn(values_t[h * DH : (h + 1) * DH], probs_b[h]) for h in range(H)], axis=0).T
    gated = (gate * attended).astype(bf16)
    up_b = upstream.astype(bf16)
    grad_gated = nn(up_b, w_out_t_ref[...])
    grad_gate = grad_gated * attended * gate * (1.0 - gate)
    grad_mixed = (grad_gated * gate).astype(bf16)
    grad_value = jnp.zeros((N, C), f32)
    grad_key = jnp.zeros((N, C), f32)
    grad_query_t = []
    for h in range(H):
        grad_probs = nt(values_h[h], grad_mixed)
        inner = jnp.sum(probs[h] * grad_probs, axis=0, keepdims=True)
        grad_scores = probs[h] * (grad_probs - inner)
        if r == 0:
            bias_sum[h] = grad_scores
        else:
            bias_sum[h] += grad_scores
        scores_b = grad_scores.astype(bf16)
        grad_value = jnp.where(masks[h], nn(probs_b[h], grad_mixed), grad_value)
        grad_key = jnp.where(masks[h], nn(scores_b, queries), grad_key)
        grad_query_t.append(nn(keys_t[h * DH : (h + 1) * DH], scores_b))
    grad_query = jnp.concatenate(grad_query_t, axis=0).T * DH ** (-0.5)
    grad_proj = jnp.concatenate([grad_query, grad_key, grad_value, grad_gate], axis=-1).astype(bf16)
    win = nn(normed.T.astype(bf16), grad_proj)
    wout = nn(gated.astype(f32).T.astype(bf16), up_b)
    blocks = [win[:, q * C : (q + 1) * C] for q in range(4)] + [wout]
    for q, block in enumerate(blocks):
        if r == 0:
            weight_sum[q] = block
        else:
            weight_sum[q] += block
    grad_normed = nn(grad_proj, w_in_t_ref[...])
    centred = (
        grad_normed
        - jnp.mean(grad_normed, axis=-1, keepdims=True)
        - normed * jnp.mean(grad_normed * normed, axis=-1, keepdims=True)
    )
    return upstream + inv_std * centred


BIAS_ROWS = R * H * N // C
WEIGHT_ROWS = 16
WEIGHT_BLOCKS = 5


def pack_terms(bias_sum, weight_sum, bias_packed, weight_packed, bias_send, weight_send):
    eye = (lax.broadcasted_iota(jnp.int32, (N, N), 0) == lax.broadcasted_iota(jnp.int32, (N, N), 1)).astype(bf16)
    halves = N // C
    for h in range(H):
        by_query = nt(eye, bias_sum[h].astype(bf16))
        for half in range(halves):
            bias_packed[pl.ds(h * halves + half, N, stride=H * halves), :] = by_query[:, half * C : (half + 1) * C]
    bias_send[...] = bias_packed[...].reshape(PEERS, BIAS_ROWS, C).astype(bf16)
    weight_packed[...] = jnp.zeros_like(weight_packed)
    for q in range(WEIGHT_BLOCKS):
        for parity in range(2):
            block = weight_sum.at[q][pl.ds(parity, PEERS, stride=2), :]
            weight_packed[pl.ds(q * 2 + parity, PEERS, stride=WEIGHT_ROWS), :] = block
    weight_send[...] = weight_packed[...].reshape(PEERS, WEIGHT_ROWS, C).astype(bf16)


def end_kernel(
    recv_ref, bias_ref, pen_ref, w_in_ref, w_in_t_ref, w_out_ref, w_out_t_ref,
    send_ref, bias_send, weight_send,
    x_all, up_all, stage, grad_packed, bias_sum, weight_sum, bias_packed, weight_packed,
):
    masks = head_masks()
    penalty = jnp.broadcast_to(pen_ref[...], (N, N))
    x_all[...] = recv_ref[:, : R * R, :].astype(f32).reshape(N * R, C)
    up_all[...] = recv_ref[:, R * R :, :].astype(f32).reshape(N * R, C)
    for r in range(R):
        grad = node_backward(
            r, x_all[pl.ds(r, N, stride=R), :], up_all[pl.ds(r, N, stride=R), :],
            bias_ref, penalty, w_in_ref, w_in_t_ref, w_out_ref, w_out_t_ref, masks, bias_sum, weight_sum,
        )
        pack_rows(grad, r, stage, grad_packed)
    send_ref[...] = grad_packed[...].reshape(PEERS, R * R, C).astype(bf16)
    pack_terms(bias_sum, weight_sum, bias_packed, weight_packed, bias_send, weight_send)


def start_kernel(
    x_ref, recv_ref, bias_ref, pen_ref, w_in_ref, w_in_t_ref, w_out_ref, w_out_t_ref,
    grad_ref, bias_send, weight_send,
    up_all, bias_sum, weight_sum, bias_packed, weight_packed,
):
    masks = head_masks()
    penalty = jnp.broadcast_to(pen_ref[...], (N, N))
    up_all[...] = recv_ref[...].astype(f32).reshape(N * R, C)
    for r in range(R):
        grad = node_backward(
            r, x_ref[r].astype(f32), up_all[pl.ds(r, N, stride=R), :],
            bias_ref, penalty, w_in_ref, w_in_t_ref, w_out_ref, w_out_t_ref, masks, bias_sum, weight_sum,
        )
        grad_ref[r] = grad.astype(bf16)
    pack_terms(bias_sum, weight_sum, bias_packed, weight_packed, bias_send, weight_send)


def sum_kernel(recv_ref, out_ref):
    out_ref[...] = jnp.sum(recv_ref[...].astype(f32), axis=0)


def weight_sum_kernel(end_ref, start_ref, out_ref):
    for part, ref in enumerate((end_ref, start_ref)):
        total = jnp.sum(ref[...].astype(f32), axis=0).astype(bf16)
        out_ref[:, part * WEIGHT_ROWS : (part + 1) * WEIGHT_ROWS, :] = jnp.broadcast_to(
            total[None], (PEERS, WEIGHT_ROWS, C)
        )


def weight_unpack_kernel(recv_ref, in_start, out_start, in_end, out_end, stage, block):
    for part, (win, wout) in enumerate(((in_end, out_end), (in_start, out_start))):
        received = recv_ref[:, part * WEIGHT_ROWS : (part + 1) * WEIGHT_ROWS, :]
        stage[...] = received.astype(f32).reshape(PEERS * WEIGHT_ROWS, C) * (1.0 / N)
        for q in range(WEIGHT_BLOCKS):
            for parity in range(2):
                block[pl.ds(parity, PEERS, stride=2), :] = stage[pl.ds(q * 2 + parity, PEERS, stride=WEIGHT_ROWS), :]
            if q < 4:
                win[:, q * C : (q + 1) * C] = block[...]
            else:
                wout[...] = block[...]


def call(kernel, outs, scratch=()):
    vmem = pl.BlockSpec(memory_space=pltpu.VMEM)
    return pl.pallas_call(
        kernel,
        out_shape=outs,
        out_specs=jax.tree.map(lambda _: vmem, outs),
        scratch_shapes=list(scratch),
        compiler_params=pltpu.CompilerParams(vmem_limit_bytes=VMEM_LIMIT),
    )


def struct(shape, dtype):
    return jax.ShapeDtypeStruct(shape, dtype)


def exchange(value):
    return lax.all_to_all(value, "dap", split_axis=0, concat_axis=0, tiled=True)


TERM_SCRATCH = (
    pltpu.VMEM((H, N, N), f32),
    pltpu.VMEM((WEIGHT_BLOCKS, C, C), f32),
    pltpu.VMEM((N * H * N // C, C), f32),
    pltpu.VMEM((PEERS * WEIGHT_ROWS, C), f32),
)
TERM_OUTS = (struct((PEERS, BIAS_ROWS, C), bf16), struct((PEERS, WEIGHT_ROWS, C), bf16))


def shards(
    pair_act,
    cotangent,
    bias_start,
    bias_end,
    w_in_start,
    w_out_start,
    w_in_end,
    w_out_end,
    residue_mask,
    window_offset,
):
    window = lax.dynamic_slice_in_dim(residue_mask, window_offset[0], N)
    penalty = ((window.astype(f32) - 1.0) * MASK_PENALTY)[:, None]
    bias_start_t = jnp.transpose(bias_start, (1, 2, 0))
    bias_end_t = jnp.transpose(bias_end, (1, 2, 0))
    rows_f32 = pltpu.VMEM((N * R, C), f32)
    stage = pltpu.VMEM((N, C), f32)

    send = call(start_forward_kernel, struct((PEERS, 2 * R * R, C), bf16), (stage, rows_f32, rows_f32))(
        pair_act, cotangent, bias_start_t, penalty, w_in_start, w_out_start
    )
    recv = exchange(send)
    grad_send, bias_end_send, weight_end_send = call(
        end_kernel,
        (struct((PEERS, R * R, C), bf16),) + TERM_OUTS,
        (rows_f32, rows_f32, stage, rows_f32) + TERM_SCRATCH,
    )(recv, bias_end_t, penalty, w_in_end, w_in_end.T, w_out_end, w_out_end.T)
    grad_recv = exchange(grad_send)
    end_terms = exchange(jnp.concatenate([bias_end_send, weight_end_send], axis=1))
    grad_pair, bias_start_send, weight_start_send = call(
        start_kernel,
        (struct((R, N, C), bf16),) + TERM_OUTS,
        (rows_f32,) + TERM_SCRATCH,
    )(pair_act, grad_recv, bias_start_t, penalty, w_in_start, w_in_start.T, w_out_start, w_out_start.T)
    weight_start_recv = exchange(weight_start_send)
    bias_start_recv = exchange(bias_start_send)
    weight_send = call(weight_sum_kernel, struct((PEERS, 2 * WEIGHT_ROWS, C), bf16))(
        end_terms[:, BIAS_ROWS:], weight_start_recv
    )
    weight_recv = exchange(weight_send)
    grad_bias_end = call(sum_kernel, struct((BIAS_ROWS, C), f32))(end_terms[:, :BIAS_ROWS])
    grad_bias_start = call(sum_kernel, struct((BIAS_ROWS, C), f32))(bias_start_recv)
    weights = call(
        weight_unpack_kernel,
        tuple(struct(shape, f32) for shape in ((C, 4 * C), (C, C), (C, 4 * C), (C, C))),
        (pltpu.VMEM((PEERS * WEIGHT_ROWS, C), f32), pltpu.VMEM((C, C), f32)),
    )(weight_recv)
    return (
        grad_pair,
        grad_bias_start.reshape(R, H, N),
        grad_bias_end.reshape(R, H, N),
    ) + tuple(weights)


def solution(mesh):
    rows = P(("dp", "dap"), None, None)
    placed = (rows, rows, P("dp", None, None), P("dp", None, None), P(), P(), P(), P(), P("dp"), P("dp"))
    return jax.shard_map(
        shards,
        mesh=mesh,
        in_specs=placed,
        out_specs=(rows, rows, rows, P("dp", None), P("dp", None), P("dp", None), P("dp", None)),
        check_vma=False,
    )
```

time: 725 us -> 195 us (0.27)
  waiting for transfers between devices: 563 us -> 80 us
  matrix products: 46.3 us -> 0 us
  local copies, waits for them, and re-layouts: 39.5 us -> 3.9 us
  Pallas kernels: 0 us -> 31.4 us
  blocking collectives: 0 us -> 29.9 us
  other arithmetic: 19.9 us -> 0.83 us
  between operations: 15.8 us -> 1.49 us
  starting transfers between devices: 37.2 us -> 46.6 us
    unnamed x2 -> x0, waiting for transfers between devices: 546 us -> none
    all_to_all x3 -> x5, waiting for transfers between devices: 17.6 us -> 80 us  [exchange(): return lax.all_to_all(value, 'dap', split_axis=0, concat_axis=0, tiled=True)]
    dot_general x21 -> x0, matrix products: 35.6 us -> none  [product(): jnp.einsum(formula, first_operand, second_operand, preferred_element_type...]
    pallas_call x0 -> x7, Pallas kernels: none -> 31.4 us  [the longest x1 10.8 us: shards(): call(start_kernel, (struct((R, N, C), bf16),) + TERM_OUTS, (rows_f32,) +...]
    all_to_all x0 -> x1, blocking collectives: none -> 29.9 us  [exchange(): return lax.all_to_all(value, 'dap', split_axis=0, concat_axis=0, tiled=True)]
    convert_element_type x9 -> x0, local copies, waits for them, and re-layouts: 11.6 us -> none  [the longest x2 4.85 us: softmax_rows(): pair_bias.astype(jnp.float32)[None]]
    sub x2 -> x0, matrix products: 10.7 us -> none  [softmax_rows(): exponent = jnp.exp(scores - row_peak)]
    all_to_all x3 -> x5, starting transfers between devices: 36.9 us -> 46.6 us  [exchange(): return lax.all_to_all(value, 'dap', split_axis=0, concat_axis=0, tiled=True)]
  transfers between devices with their start and end apart: 4 -> 5, of which waited for: 3 -> 5; matrix products, arithmetic and copies ran while one was open for 4% -> 1% of each run, Pallas kernels for 0% -> 1%
where the time goes in v1:
time: 195 us; the launch traced here: 194 us
  waiting for transfers between devices  80 us (41%)
  starting transfers between devices  46.6 us (24%)
  Pallas kernels  31.4 us (16%)
  blocking collectives  29.9 us (15%)
  local copies, waits for them, and re-layouts  3.9 us (2%)
    all_to_all x5, waiting for transfers between devices, exchange(): return lax.all_to_all(value, 'dap', split_axis=0, concat_axis=0, tiled=True)  80 us
    all_to_all x5, starting transfers between devices, exchange(): return lax.all_to_all(value, 'dap', split_axis=0, concat_axis=0, tiled=True)  46.6 us
    all_to_all x1, blocking collectives, exchange(): return lax.all_to_all(value, 'dap', split_axis=0, concat_axis=0, tiled=True)  29.9 us
    pallas_call x1, Pallas kernels, shards(): call(start_kernel, (struct((R, N, C), bf16),) + TERM_OUTS, (rows_f32,) +...  10.8 us
    pallas_call x1, Pallas kernels, shards(): call(end_kernel, (struct((PEERS, R * R, C), bf16),) + TERM_OUTS, (rows_f3...  10.8 us
    pallas_call x1, Pallas kernels, shards(): call(start_forward_kernel, struct((PEERS, 2 * R * R, C), bf16), (stage, r...  7.43 us
  transfers between devices with their start and end apart: 5, of which 5 were waited for; matrix products, arithmetic and copies ran while one was open for 1% of the time, Pallas kernels for 1%

profile of v1, /device:TPU:1, one launch (start us, length us, event | category | flops | bytes accessed | tf_op | source)
XLA Modules:
  0.0 194.0 jit_solution(16845391647729409087)
XLA Ops:
  0.7 1.4 copy.23
  2.7 0.8 add_multiply_fusion
  3.5 0.1 copy.24.pen_ref
  3.7 7.4 %shard_map.153 = bf16[64,32,128]{2,1,0:T(8,128)(2,1)} custom-call(bf16[4,256,128]{2,1,0:T(8,128)(2,1)S(1)} %copy-done.1, bf16[4,256,128]{2,1,0:T(8,128)(2,1)S(1)} %copy-done.4, bf16[4,256,256]{2,1,0:T(8,128)(2,1)S(1)} %bitcast.11, f32[256,1]{1,0:T(8,128)S(1)} %copy.24.pen_ref, bf16[128,512]{1,0:T(8,128)(2,1)S(1)} %copy-done, bf16[128,128]{1,0:T(8,128)(2,1)S(1)} %copy-done.3), custom_call_target="tpu_custom_call" | custom-call | tf_op jit(solution)/shard_map/pallas_call | solution.py:278
  11.1 17.8 %all-to-all-start = ((bf16[64,32,128]{2,1,0:T(8,128)(2,1)}), bf16[64,32,128]{2,1,0:T(8,128)(2,1)S(1)}, u32[]{:S(2)}, u32[]{:S(2)}) async-start(bf16[64,32,128]{2,1,0:T(8,128)(2,1)} %shard_map.153), calls=%async_computation | async-start | bytes 1048576 | tf_op jit(solution)/shard_map/all_to_all | solution.py:247
  28.9 0.3 copy.25
  29.2 0.1 copy.26
  29.4 0.3 copy-done.5
  29.8 17.8 %all-to-all-done.recv_ref = bf16[64,32,128]{2,1,0:T(8,128)(2,1)S(1)} async-done(((bf16[64,32,128]{2,1,0:T(8,128)(2,1)}), bf16[64,32,128]{2,1,0:T(8,128)(2,1)S(1)}, u32[]{:S(2)}, u32[]{:S(2)}) %all-to-all-start) | async-done | bytes 524320 | tf_op jit(solution)/shard_map/all_to_all | solution.py:247
  47.6 10.8 %shard_map.154 = (bf16[64,16,128]{2,1,0:T(8,128)(2,1)}, bf16[64,32,128]{2,1,0:T(8,128)(2,1)S(1)}, bf16[64,16,128]{2,1,0:T(8,128)(2,1)S(1)}) custom-call(bf16[64,32,128]{2,1,0:T(8,128)(2,1)S(1)} %all-to-all-done.recv_ref, bf16[4,256,256]{2,1,0:T(8,128)(2,1)S(1)} %bitcast.13, f32[256,1]{1,0:T(8,128)S(1)} %copy.24.pen_ref, bf16[128,512]{1,0:T(8,128)(2,1)S(1)} %copy-done.2, ...), custom_call_target="tpu_custom_call" | custom-call | tf_op jit(solution)/shard_map/pallas_call | solution.py:282
  58.4 7.7 %all-to-all-start.1 = ((bf16[64,16,128]{2,1,0:T(8,128)(2,1)}), bf16[64,16,128]{2,1,0:T(8,128)(2,1)S(1)}, u32[]{:S(2)}, u32[]{:S(2)}) async-start(bf16[64,16,128]{2,1,0:T(8,128)(2,1)} %get-tuple-element.17), calls=%async_computation.1 | async-start | bytes 524288 | tf_op jit(solution)/shard_map/all_to_all | solution.py:247
  66.3 13.6 %all-to-all-done.1.recv_ref = bf16[64,16,128]{2,1,0:T(8,128)(2,1)S(1)} async-done(((bf16[64,16,128]{2,1,0:T(8,128)(2,1)}), bf16[64,16,128]{2,1,0:T(8,128)(2,1)S(1)}, u32[]{:S(2)}, u32[]{:S(2)}) %all-to-all-start.1) | async-done | bytes 262176 | tf_op jit(solution)/shard_map/all_to_all | solution.py:247
  79.9 10.8 %shard_map.155 = (bf16[4,256,128]{2,1,0:T(8,128)(2,1)}, bf16[64,32,128]{2,1,0:T(8,128)(2,1)}, bf16[64,16,128]{2,1,0:T(8,128)(2,1)}) custom-call(bf16[4,256,128]{2,1,0:T(8,128)(2,1)S(1)} %copy-done.1, bf16[64,16,128]{2,1,0:T(8,128)(2,1)S(1)} %all-to-all-done.1.recv_ref, bf16[4,256,256]{2,1,0:T(8,128)(2,1)S(1)} %bitcast.12, f32[256,1]{1,0:T(8,128)S(1)} %copy.24.pen_ref, ...), custom_call_target="tpu_custom_call" | custom-call | tf_op jit(solution)/shard_map/pallas_call | solution.py:289
  90.7 6.2 %all-to-all-start.4 = ((bf16[64,16,128]{2,1,0:T(8,128)(2,1)}), bf16[64,16,128]{2,1,0:T(8,128)(2,1)S(1)}, u32[]{:S(2)}, u32[]{:S(2)}) async-start(bf16[64,16,128]{2,1,0:T(8,128)(2,1)} %get-tuple-element.22), calls=%async_computation.4 | async-start | bytes 524288 | tf_op jit(solution)/shard_map/all_to_all | solution.py:247
  96.9 13.8 %all-to-all-done.4.start_ref = bf16[64,16,128]{2,1,0:T(8,128)(2,1)S(1)} async-done(((bf16[64,16,128]{2,1,0:T(8,128)(2,1)}), bf16[64,16,128]{2,1,0:T(8,128)(2,1)S(1)}, u32[]{:S(2)}, u32[]{:S(2)}) %all-to-all-start.4) | async-done | bytes 262176 | tf_op jit(solution)/shard_map/all_to_all | solution.py:247
  110.7 29.9 %all_to_all.30 = bf16[64,48,128]{2,1,0:T(8,128)(2,1)S(1)} all-to-all(bf16[64,48,128]{2,1,0:T(8,128)(2,1)S(1)} %pad_maximum_fusion), channel_id=1, replica_groups=mesh['dp'=8,'dap'=64] {'dap'}, dimensions={0} | all-to-all | bytes 1572864 | tf_op jit(solution)/shard_map/all_to_all | solution.py:247
  140.6 7.7 %all-to-all-start.2 = ((bf16[64,32,128]{2,1,0:T(8,128)(2,1)}), bf16[64,32,128]{2,1,0:T(8,128)(2,1)S(1)}, u32[]{:S(2)}, u32[]{:S(2)}) async-start(bf16[64,32,128]{2,1,0:T(8,128)(2,1)} %get-tuple-element.19), calls=%async_computation.2 | async-start | bytes 1048576 | tf_op jit(solution)/shard_map/all_to_all | solution.py:247
  148.4 0.9 shard_map.158
  149.3 17.7 %all-to-all-done.2.recv_ref = bf16[64,32,128]{2,1,0:T(8,128)(2,1)S(1)} async-done(((bf16[64,32,128]{2,1,0:T(8,128)(2,1)}), bf16[64,32,128]{2,1,0:T(8,128)(2,1)S(1)}, u32[]{:S(2)}, u32[]{:S(2)}) %all-to-all-start.2) | async-done | bytes 524320 | tf_op jit(solution)/shard_map/all_to_all | solution.py:247
  166.9 7.3 %all-to-all-start.5 = ((bf16[64,32,128]{2,1,0:T(8,128)(2,1)}), bf16[64,32,128]{2,1,0:T(8,128)(2,1)S(1)}, u32[]{:S(2)}, u32[]{:S(2)}) async-start(bf16[64,32,128]{2,1,0:T(8,128)(2,1)} %shard_map.158), calls=%async_computation.5 | async-start | bytes 1048576 | tf_op jit(solution)/shard_map/all_to_all | solution.py:247
  174.4 0.6 reshape.20
  175.1 0.6 reshape.21
  175.7 17.1 %all-to-all-done.5.recv_ref = bf16[64,32,128]{2,1,0:T(8,128)(2,1)S(1)} async-done(((bf16[64,32,128]{2,1,0:T(8,128)(2,1)}), bf16[64,32,128]{2,1,0:T(8,128)(2,1)S(1)}, u32[]{:S(2)}, u32[]{:S(2)}) %all-to-all-start.5) | async-done | bytes 524320 | tf_op jit(solution)/shard_map/all_to_all | solution.py:247
  192.8 1.2 shard_map.159
  (21 shorter events, 0.7 us)
Async XLA Ops:
  0.6 3.0 %copy-start.1 = (bf16[4,256,128]{2,1,0:T(8,128)(2,1)S(1)}, bf16[4,256,128]{2,1,0:T(8,128)(2,1)}, u32[]{:S(2)}) copy-start(bf16[4,256,128]{2,1,0:T(8,128)(2,1)} %x_ref.3) | copy-start | bytes 786436
  0.6 3.0 %copy-start.4 = (bf16[4,256,128]{2,1,0:T(8,128)(2,1)S(1)}, bf16[4,256,128]{2,1,0:T(8,128)(2,1)}, u32[]{:S(2)}) copy-start(bf16[4,256,128]{2,1,0:T(8,128)(2,1)} %cot_ref.1) | copy-start | bytes 786436
  0.7 3.0 %copy-start = (bf16[128,512]{1,0:T(8,128)(2,1)S(1)}, bf16[128,512]{1,0:T(8,128)(2,1)}, u32[]{:S(2)}) copy-start(bf16[128,512]{1,0:T(8,128)(2,1)} %w_in_ref.5) | copy-start | bytes 393220
  0.7 3.0 %copy-start.3 = (bf16[128,128]{1,0:T(8,128)(2,1)S(1)}, bf16[128,128]{1,0:T(8,128)(2,1)}, u32[]{:S(2)}) copy-start(bf16[128,128]{1,0:T(8,128)(2,1)} %w_out_ref.5) | copy-start | bytes 98308
  11.1 17.8 %copy-start.6 = (bf16[256,4,256]{2,1,0:T(4,128)(2,1)S(1)}, bf16[256,4,256]{2,1,0:T(4,128)(2,1)}, u32[]{:S(2)}) copy-start(bf16[256,4,256]{2,1,0:T(4,128)(2,1)} %param.13) | copy-start | bytes 1572868
  11.1 18.1 %copy-start.2 = (bf16[128,512]{1,0:T(8,128)(2,1)S(1)}, bf16[128,512]{1,0:T(8,128)(2,1)}, u32[]{:S(2)}) copy-start(bf16[128,512]{1,0:T(8,128)(2,1)} %w_in_ref.4) | copy-start | bytes 393220
  11.1 36.5 %all-to-all-start = ((bf16[64,32,128]{2,1,0:T(8,128)(2,1)}), bf16[64,32,128]{2,1,0:T(8,128)(2,1)S(1)}, u32[]{:S(2)}, u32[]{:S(2)}) async-start(bf16[64,32,128]{2,1,0:T(8,128)(2,1)} %shard_map.153), calls=%async_computation | async-start | bytes 1048576 | tf_op jit(solution)/shard_map/all_to_all | solution.py:247
  28.9 0.8 copy-start.5
  58.4 21.5 %all-to-all-start.1 = ((bf16[64,16,128]{2,1,0:T(8,128)(2,1)}), bf16[64,16,128]{2,1,0:T(8,128)(2,1)S(1)}, u32[]{:S(2)}, u32[]{:S(2)}) async-start(bf16[64,16,128]{2,1,0:T(8,128)(2,1)} %get-tuple-element.17), calls=%async_computation.1 | async-start | bytes 524288 | tf_op jit(solution)/shard_map/all_to_all | solution.py:247
  90.7 20.0 %all-to-all-start.4 = ((bf16[64,16,128]{2,1,0:T(8,128)(2,1)}), bf16[64,16,128]{2,1,0:T(8,128)(2,1)S(1)}, u32[]{:S(2)}, u32[]{:S(2)}) async-start(bf16[64,16,128]{2,1,0:T(8,128)(2,1)} %get-tuple-element.22), calls=%async_computation.4 | async-start | bytes 524288 | tf_op jit(solution)/shard_map/all_to_all | solution.py:247
  140.6 26.3 %all-to-all-start.2 = ((bf16[64,32,128]{2,1,0:T(8,128)(2,1)}), bf16[64,32,128]{2,1,0:T(8,128)(2,1)S(1)}, u32[]{:S(2)}, u32[]{:S(2)}) async-start(bf16[64,32,128]{2,1,0:T(8,128)(2,1)} %get-tuple-element.19), calls=%async_computation.2 | async-start | bytes 1048576 | tf_op jit(solution)/shard_map/all_to_all | solution.py:247
  166.9 25.9 %all-to-all-start.5 = ((bf16[64,32,128]{2,1,0:T(8,128)(2,1)}), bf16[64,32,128]{2,1,0:T(8,128)(2,1)S(1)}, u32[]{:S(2)}, u32[]{:S(2)}) async-start(bf16[64,32,128]{2,1,0:T(8,128)(2,1)} %shard_map.158), calls=%async_computation.5 | async-start | bytes 1048576 | tf_op jit(solution)/shard_map/all_to_all | solution.py:247

commit v2 on v1

v2 whole, which is shorter than its diff:
```python
import functools

import jax
import jax.numpy as jnp
from jax import lax
from jax.experimental import pallas as pl
from jax.experimental.pallas import tpu as pltpu
from jax.sharding import PartitionSpec as P

H = 4
DH = 32
N = 256
C = 128
R = 4
PEERS = N // R

LN_EPSILON = 1e-05
MASK_PENALTY = 1000000000.0

f32 = jnp.float32
bf16 = jnp.bfloat16

VMEM_LIMIT = 40 * 1024 * 1024

GROUP = 4


def dot(a, b, dims):
    return lax.dot_general(a, b, (dims, ((), ())), preferred_element_type=f32)


def nn(a, b):
    return dot(a, b, ((1,), (0,)))


def nt(a, b):
    return dot(a, b, ((1,), (1,)))


def head_masks():
    lane = lax.broadcasted_iota(jnp.int32, (N, C), 1) // DH
    return [lane == h for h in range(H)]


def masked(value, masks):
    zero = jnp.zeros_like(value)
    return [jnp.where(m, value, zero) for m in masks]


def layer_stats(values):
    centred = values - jnp.mean(values, axis=-1, keepdims=True)
    inv_std = lax.rsqrt(jnp.mean(centred * centred, axis=-1, keepdims=True) + LN_EPSILON)
    return centred * inv_std, inv_std


def project(normed, w_in):
    projected = nn(normed, w_in)
    queries = (projected[:, :C] * DH ** (-0.5)).astype(bf16)
    keys = projected[:, C : 2 * C].astype(bf16)
    values = projected[:, 2 * C : 3 * C].astype(bf16)
    gate = 1.0 / (1.0 + jnp.exp(-projected[:, 3 * C :]))
    return queries, keys, values, gate


def pack_rows(value, r, stage, packed):
    stage[...] = value
    for residue in range(R):
        packed[pl.ds(r * R + residue, PEERS, stride=R * R), :] = stage[pl.ds(residue, PEERS, stride=R), :]


def softmax_all(keys_h, queries, bias_ref, penalty):
    scores = [[nt(keys_h[r][h], queries[r]) for h in range(H)] for r in range(len(queries))]
    return [[head_softmax(row[h], bias_ref[h], penalty) for h in range(H)] for row in scores]


def head_softmax(scores, bias_h, penalty):
    scores = scores + bias_h.astype(f32) + penalty
    exponent = jnp.exp(scores - jnp.max(scores, axis=0, keepdims=True))
    return exponent * (1.0 / jnp.sum(exponent, axis=0, keepdims=True))


def attend_all(values_t, probs_b):
    parts = [
        [nn(values_t[r][h * DH : (h + 1) * DH], probs_b[r][h]) for h in range(H)] for r in range(len(values_t))
    ]
    return [jnp.concatenate(row, axis=0).T for row in parts]


def start_forward_kernel(x_ref, cot_ref, bias_ref, pen_ref, w_in_ref, w_out_ref, send_ref, stage, first_packed, cot_packed):
    masks = head_masks()
    penalty = jnp.broadcast_to(pen_ref[...], (N, N))
    x = x_ref[...].reshape(R * N, C).astype(f32)
    normed, _ = layer_stats(x)
    queries, keys, values, gate = project(normed.astype(bf16), w_in_ref[...])
    attended = []
    for first in range(0, R, GROUP):
        rows = [slice(r * N, (r + 1) * N) for r in range(first, first + GROUP)]
        keys_h = [masked(keys[at], masks) for at in rows]
        values_t = [values[at].astype(f32).T.astype(bf16) for at in rows]
        probs = softmax_all(keys_h, [queries[at] for at in rows], bias_ref, penalty)
        attended += attend_all(values_t, [[p.astype(bf16) for p in row] for row in probs])
    gated = (gate * jnp.concatenate(attended, axis=0)).astype(bf16)
    out = (x + nn(gated, w_out_ref[...])).astype(bf16).astype(f32)
    for r in range(R):
        pack_rows(out[r * N : (r + 1) * N], r, stage.at[r], first_packed)
        pack_rows(cot_ref[r].astype(f32), r, stage.at[R + r], cot_packed)
    send_ref[:, : R * R, :] = first_packed[...].reshape(PEERS, R * R, C).astype(bf16)
    send_ref[:, R * R :, :] = cot_packed[...].reshape(PEERS, R * R, C).astype(bf16)


def node_states(x, bias_ref, penalty, w_in_ref, masks):
    count = x.shape[0] // N
    normed, inv_std = layer_stats(x)
    queries, keys, values, gate = project(normed.astype(bf16), w_in_ref[...])
    rows = [slice(r * N, (r + 1) * N) for r in range(count)]
    keys_h = [masked(keys[at], masks) for at in rows]
    values_t = [values[at].astype(f32).T.astype(bf16) for at in rows]
    keys_t = [keys[at].astype(f32).T.astype(bf16) for at in rows]
    probs = softmax_all(keys_h, [queries[at] for at in rows], bias_ref, penalty)
    attended = attend_all(values_t, [[p.astype(bf16) for p in row] for row in probs])
    return [
        (normed[at], inv_std[at], queries[at], keys_t[r], values[at], gate[at], attended[r], probs[r])
        for r, at in enumerate(rows)
    ]


def node_backward(first, states, upstreams, w_in_t_ref, w_out_t_ref, masks, bias_sum, weight_sum):
    count = len(states)
    normed, inv_std, queries, keys_t, values, gate, attended, probs = zip(*states)
    values_h = [masked(v, masks) for v in values]
    up_b = [u.astype(bf16) for u in upstreams]
    grad_gated = [nn(u, w_out_t_ref[...]) for u in up_b]
    gated = [(gate[r] * attended[r]).astype(bf16) for r in range(count)]
    grad_gate = [grad_gated[r] * attended[r] * gate[r] * (1.0 - gate[r]) for r in range(count)]
    grad_mixed = [(grad_gated[r] * gate[r]).astype(bf16) for r in range(count)]
    grad_probs = [[nt(values_h[r][h], grad_mixed[r]) for h in range(H)] for r in range(count)]
    scores_b = [[None] * H for _ in range(count)]
    for h in range(H):
        total = None
        for r in range(count):
            inner = jnp.sum(probs[r][h] * grad_probs[r][h], axis=0, keepdims=True)
            grad_scores = probs[r][h] * (grad_probs[r][h] - inner)
            scores_b[r][h] = grad_scores.astype(bf16)
            total = grad_scores if total is None else total + grad_scores
        if first:
            bias_sum[h] = total
        else:
            bias_sum[h] += total
    wins, wouts, grads = [], [], []
    by_value = [[nn(probs[r][h].astype(bf16), grad_mixed[r]) for h in range(H)] for r in range(count)]
    by_key = [[nn(scores_b[r][h], queries[r]) for h in range(H)] for r in range(count)]
    by_query = [[nn(keys_t[r][h * DH : (h + 1) * DH], scores_b[r][h]) for h in range(H)] for r in range(count)]
    for r in range(count):
        grad_value, grad_key = by_value[r][0], by_key[r][0]
        for h in range(1, H):
            grad_value = jnp.where(masks[h], by_value[r][h], grad_value)
            grad_key = jnp.where(masks[h], by_key[r][h], grad_key)
        grad_query = jnp.concatenate(by_query[r], axis=0).T * DH ** (-0.5)
        grad_proj = jnp.concatenate([grad_query, grad_key, grad_value, grad_gate[r]], axis=-1).astype(bf16)
        wins.append(nn(normed[r].T.astype(bf16), grad_proj))
        wouts.append(nn(gated[r].astype(f32).T.astype(bf16), up_b[r]))
        grad_normed = nn(grad_proj, w_in_t_ref[...])
        centred = (
            grad_normed
            - jnp.mean(grad_normed, axis=-1, keepdims=True)
            - normed[r] * jnp.mean(grad_normed * normed[r], axis=-1, keepdims=True)
        )
        grads.append(upstreams[r] + inv_std[r] * centred)
    win, wout = sum(wins[1:], wins[0]), sum(wouts[1:], wouts[0])
    blocks = [win[:, q * C : (q + 1) * C] for q in range(4)] + [wout]
    for q, block in enumerate(blocks):
        if first:
            weight_sum[q] = block
        else:
            weight_sum[q] += block
    return grads


CHUNKS = H * N // C
WEIGHT_BLOCKS = 5
BIAS_HALF = 2 * PEERS * CHUNKS
WEIGHT_HALF = WEIGHT_BLOCKS * PEERS
SEND_ROWS = 32
WEIGHT_ROWS = 16


def core_index():
    return lax.axis_index("dap") % 2


def row_parity():
    return (lax.axis_index("dap") // 2) % 2


def split_bias(bias_sum, bias_packed, core):
    eye = (lax.broadcasted_iota(jnp.int32, (N, N), 0) == lax.broadcasted_iota(jnp.int32, (N, N), 1)).astype(bf16)
    for h in range(H):
        by_query = nt(eye, bias_sum[h].astype(bf16))
        for half in range(N // C):
            bias_packed[pl.ds(half * H + h, N, stride=CHUNKS), :] = by_query[:, half * C : (half + 1) * C]
    terms = bias_packed[...].reshape(PEERS, R, CHUNKS, C)
    keep, give = [], []
    for parity in range(2):
        even, odd = terms[:, 2 * parity], terms[:, 2 * parity + 1]
        keep.append(jnp.where(core == 0, even, odd).reshape(PEERS * CHUNKS, C))
        give.append(jnp.where(core == 0, odd, even).reshape(PEERS * CHUNKS, C))
    return keep, give


def end_kernel(
    recv_ref, bias_ref, pen_ref, w_in_ref, w_in_t_ref, w_out_t_ref,
    send_ref, give_ref, keep_ref,
    x_all, up_all, stage, grad_packed, bias_sum, weight_sum, bias_packed,
):
    masks = head_masks()
    core = core_index()
    penalty = jnp.broadcast_to(pen_ref[...], (N, N))
    x_all[...] = recv_ref[:, : R * R, :].astype(f32).reshape(N * R, C)
    up_all[...] = recv_ref[:, R * R :, :].astype(f32).reshape(N * R, C)
    for first in range(0, R, GROUP):
        group = range(first, first + GROUP)
        x = jnp.concatenate([x_all[pl.ds(r, N, stride=R), :] for r in group], axis=0)
        states = node_states(x, bias_ref, penalty, w_in_ref, masks)
        upstreams = [up_all[pl.ds(r, N, stride=R), :] for r in group]
        grads = node_backward(first == 0, states, upstreams, w_in_t_ref, w_out_t_ref, masks, bias_sum, weight_sum)
        for r, grad in zip(group, grads):
            pack_rows(grad, r, stage.at[r], grad_packed)
    send_ref[...] = grad_packed[...].reshape(PEERS, R * R, C).astype(bf16)
    keep, give = split_bias(bias_sum, bias_packed, core)
    for parity in range(2):
        rows = pl.ds(parity * PEERS * CHUNKS, PEERS * CHUNKS)
        keep_ref[rows, :] = keep[parity]
        give_ref[rows, :] = give[parity].astype(bf16)
    for q in range(WEIGHT_BLOCKS):
        even = weight_sum.at[q][pl.ds(0, PEERS, stride=2), :]
        odd = weight_sum.at[q][pl.ds(1, PEERS, stride=2), :]
        rows = pl.ds(BIAS_HALF + q * PEERS, PEERS)
        keep_ref[rows, :] = jnp.where(core == 0, even, odd)
        give_ref[rows, :] = jnp.where(core == 0, odd, even).astype(bf16)


def start_kernel(
    x_ref, recv_ref, bias_ref, pen_ref, w_in_ref, w_in_t_ref, w_out_t_ref, end_keep_ref, end_got_ref,
    grad_ref, send_ref, give_ref, keep_ref,
    up_all, bias_sum, weight_sum, bias_packed, weight_packed,
):
    masks = head_masks()
    core = core_index()
    penalty = jnp.broadcast_to(pen_ref[...], (N, N))
    up_all[...] = recv_ref[...].astype(f32).reshape(N * R, C)
    for first in range(0, R, GROUP):
        group = range(first, first + GROUP)
        x = x_ref[first : first + GROUP].reshape(GROUP * N, C).astype(f32)
        states = node_states(x, bias_ref, penalty, w_in_ref, masks)
        upstreams = [up_all[pl.ds(r, N, stride=R), :] for r in group]
        grads = node_backward(first == 0, states, upstreams, w_in_t_ref, w_out_t_ref, masks, bias_sum, weight_sum)
        for r, grad in zip(group, grads):
            grad_ref[r] = grad.astype(bf16)
    end_terms = end_keep_ref[...] + end_got_ref[...].astype(f32)
    weight_packed[...] = jnp.zeros_like(weight_packed)
    for q in range(WEIGHT_BLOCKS):
        for parity in range(2):
            block = weight_sum.at[q][pl.ds(parity, PEERS, stride=2), :]
            weight_packed[pl.ds(q * 2 + parity, PEERS, stride=WEIGHT_ROWS), :] = block
        block = end_terms[BIAS_HALF + q * PEERS : BIAS_HALF + (q + 1) * PEERS]
        weight_packed[pl.ds(2 * WEIGHT_BLOCKS + q, PEERS, stride=WEIGHT_ROWS), :] = block
    end_bias = [
        end_terms[parity * PEERS * CHUNKS : (parity + 1) * PEERS * CHUNKS].reshape(PEERS, CHUNKS, C)
        for parity in range(2)
    ]
    weights = weight_packed[...].reshape(PEERS, WEIGHT_ROWS, C)
    send_ref[...] = jnp.concatenate(end_bias + [weights], axis=1).astype(bf16)
    keep, give = split_bias(bias_sum, bias_packed, core)
    for parity in range(2):
        rows = pl.ds(parity * PEERS * CHUNKS, PEERS * CHUNKS)
        keep_ref[rows, :] = keep[parity]
        give_ref[rows, :] = give[parity].astype(bf16)


def pair_sum_kernel(keep_ref, got_ref, next_keep_ref, next_give_ref):
    total = keep_ref[...] + got_ref[...].astype(f32)
    low, high = total[: PEERS * CHUNKS], total[PEERS * CHUNKS :]
    parity = row_parity()
    next_keep_ref[...] = jnp.where(parity == 0, low, high)
    next_give_ref[...] = jnp.where(parity == 0, high, low).astype(bf16)


def write_bias(rows, out_ref):
    for residue in range(R):
        for half in range(N // C):
            out_ref[residue, :, half * C : (half + 1) * C] = rows[residue][half * H : (half + 1) * H]


def middle_kernel(recv_ref, keep_ref, got_ref, bias_ref, send_ref):
    by_core = jnp.sum(recv_ref[...].astype(f32).reshape(PEERS // 2, 2, SEND_ROWS, C), axis=0)
    end_bias = [by_core[core, parity * CHUNKS : (parity + 1) * CHUNKS] for parity in range(2) for core in range(2)]
    write_bias(end_bias, bias_ref)
    even, odd = by_core[0, 2 * CHUNKS :], by_core[1, 2 * CHUNKS :]
    slot = lax.broadcasted_iota(jnp.int32, (WEIGHT_ROWS, C), 0)
    totals = jnp.concatenate([even + jnp.where(slot < 2 * WEIGHT_BLOCKS, odd, 0.0), odd[CHUNKS:]], axis=0)
    bias_terms = (keep_ref[...] + got_ref[...].astype(f32)).reshape(PEERS, CHUNKS, C)
    everyone = jnp.broadcast_to(totals[None], (PEERS, SEND_ROWS - CHUNKS, C))
    send_ref[...] = jnp.concatenate([bias_terms, everyone], axis=1).astype(bf16)


def last_kernel(recv_ref, bias_ref, in_start, out_start, in_end, out_end, stage, block):
    received = recv_ref[...].astype(f32)
    write_bias(jnp.sum(received[:, :CHUNKS].reshape(PEERS // R, R, CHUNKS, C), axis=0), bias_ref)
    span = SEND_ROWS - CHUNKS
    stage[...] = received[:, CHUNKS:].reshape(PEERS * span, C) * (1.0 / N)
    end_slots = (2 * WEIGHT_BLOCKS, WEIGHT_ROWS + 2 * WEIGHT_BLOCKS - CHUNKS)
    for part, (win, wout) in enumerate(((in_start, out_start), (in_end, out_end))):
        for q in range(WEIGHT_BLOCKS):
            for parity in range(2):
                row = q * 2 + parity if part == 0 else end_slots[parity] + q
                block[pl.ds(parity, PEERS, stride=2), :] = stage[pl.ds(row, PEERS, stride=span), :]
            if q < 4:
                win[:, q * C : (q + 1) * C] = block[...]
            else:
                wout[...] = block[...]


def call(kernel, outs, scratch=(), far=()):
    vmem = pl.BlockSpec(memory_space=pltpu.VMEM)

    def apply(*operands):
        placed = [pltpu.with_memory_space_constraint(v, pltpu.HBM) if i in far else v for i, v in enumerate(operands)]
        return pl.pallas_call(
            kernel,
            out_shape=outs,
            in_specs=[vmem] * len(operands),
            out_specs=jax.tree.map(lambda _: vmem, outs),
            scratch_shapes=list(scratch),
            compiler_params=pltpu.CompilerParams(vmem_limit_bytes=VMEM_LIMIT),
        )(*placed)

    return apply


def struct(shape, dtype):
    return jax.ShapeDtypeStruct(shape, dtype)


def exchange(value):
    return lax.all_to_all(value, "dap", split_axis=0, concat_axis=0, tiled=True)


def swap(value, distance):
    return lax.ppermute(value, "dap", [(i, i ^ distance) for i in range(PEERS)])


def shards(
    pair_act,
    cotangent,
    bias_start,
    bias_end,
    w_in_start,
    w_out_start,
    w_in_end,
    w_out_end,
    residue_mask,
    window_offset,
):
    window = lax.dynamic_slice_in_dim(residue_mask, window_offset[0], N)
    penalty = ((window.astype(f32) - 1.0) * MASK_PENALTY)[:, None]
    bias_start_t = jnp.transpose(bias_start, (1, 2, 0))
    bias_end_t = jnp.transpose(bias_end, (1, 2, 0))
    rows_f32 = pltpu.VMEM((N * R, C), f32)
    bias_sum = pltpu.VMEM((H, N, N), f32)
    weight_sum = pltpu.VMEM((WEIGHT_BLOCKS, C, C), f32)
    bias_packed = pltpu.VMEM((N * CHUNKS, C), f32)
    weight_packed = pltpu.VMEM((PEERS * WEIGHT_ROWS, C), f32)
    term_rows = PEERS * CHUNKS

    send = call(start_forward_kernel, struct((PEERS, 2 * R * R, C), bf16), (pltpu.VMEM((2 * R, N, C), f32), rows_f32, rows_f32))(
        pair_act, cotangent, bias_start_t, penalty, w_in_start, w_out_start
    )
    recv = exchange(send)
    grad_send, end_give, end_keep = call(
        end_kernel,
        (
            struct((PEERS, R * R, C), bf16),
            struct((BIAS_HALF + WEIGHT_HALF, C), bf16),
            struct((BIAS_HALF + WEIGHT_HALF, C), f32),
        ),
        (rows_f32, rows_f32, pltpu.VMEM((R, N, C), f32), rows_f32, bias_sum, weight_sum, bias_packed),
    )(recv, bias_end_t, penalty, w_in_end, w_in_end.T, w_out_end.T)
    grad_recv = exchange(grad_send)
    end_got = swap(end_give, 1)
    grad_pair, term_send, start_give, start_keep = call(
        start_kernel,
        (
            struct((R, N, C), bf16),
            struct((PEERS, SEND_ROWS, C), bf16),
            struct((BIAS_HALF, C), bf16),
            struct((BIAS_HALF, C), f32),
        ),
        (rows_f32, bias_sum, weight_sum, bias_packed, weight_packed),
    )(pair_act, grad_recv, bias_start_t, penalty, w_in_start, w_in_start.T, w_out_start.T, end_keep, end_got)
    term_recv = exchange(term_send)
    pair_keep, pair_give = call(pair_sum_kernel, (struct((term_rows, C), f32), struct((term_rows, C), bf16)))(
        start_keep, swap(start_give, 1)
    )
    pair_got = swap(pair_give, 2)
    grad_bias_end, last_send = call(
        middle_kernel, (struct((R, H, N), f32), struct((PEERS, SEND_ROWS, C), bf16))
    )(term_recv, pair_keep, pair_got)
    last_recv = exchange(last_send)
    grad_bias_start, *weights = call(
        last_kernel,
        (struct((R, H, N), f32),) + tuple(struct(shape, f32) for shape in ((C, 4 * C), (C, C), (C, 4 * C), (C, C))),
        (pltpu.VMEM((PEERS * (SEND_ROWS - CHUNKS), C), f32), pltpu.VMEM((C, C), f32)),
    )(last_recv)
    return (grad_pair, grad_bias_start, grad_bias_end, *weights)


def solution(mesh):
    rows = P(("dp", "dap"), None, None)
    placed = (rows, rows, P("dp", None, None), P("dp", None, None), P(), P(), P(), P(), P("dp"), P("dp"))
    return jax.shard_map(
        shards,
        mesh=mesh,
        in_specs=placed,
        out_specs=(rows, rows, rows, P("dp", None), P("dp", None), P("dp", None), P("dp", None)),
        check_vma=False,
    )
```

time: 195 us -> 134 us (0.69)
  waiting for transfers between devices: 80 us -> 42.2 us
  Pallas kernels: 31.4 us -> 19.5 us
  starting transfers between devices: 46.6 us -> 39.7 us
  blocking collectives: 29.9 us -> 27.9 us
    all_to_all x5 -> x3, waiting for transfers between devices: 80 us -> 31 us  [exchange(): return lax.all_to_all(value, 'dap', split_axis=0, concat_axis=0, tiled=True)]
    all_to_all x5 -> x3, starting transfers between devices: 46.6 us -> 31.6 us  [exchange(): return lax.all_to_all(value, 'dap', split_axis=0, concat_axis=0, tiled=True)]
    pallas_call x7 -> x6, Pallas kernels: 31.4 us -> 19.5 us  [apply(): pl.pallas_call(kernel, out_shape=outs, in_specs=[vmem] * len(operands), o...]
    ppermute x0 -> x3, waiting for transfers between devices: none -> 11.2 us  [swap(): return lax.ppermute(value, 'dap', [(i, i ^ distance) for i in range(PEERS)])]
    ppermute x0 -> x3, starting transfers between devices: none -> 8.12 us  [swap(): return lax.ppermute(value, 'dap', [(i, i ^ distance) for i in range(PEERS)])]
    all_to_all x1, blocking collectives: 29.9 us -> 27.9 us  [exchange(): return lax.all_to_all(value, 'dap', split_axis=0, concat_axis=0, tiled=True)]
  transfers between devices with their start and end apart: 5 -> 6, of which waited for: 5 -> 6; matrix products, arithmetic and copies ran while one was open for 1% -> 1% of each run, Pallas kernels for 1% -> 0%
where the time goes in v2:
time: 134 us
  waiting for transfers between devices  42.2 us (31%)
  starting transfers between devices  39.7 us (30%)
  blocking collectives  27.9 us (21%)
  Pallas kernels  19.5 us (15%)
  local copies, waits for them, and re-layouts  2.35 us (2%)
  between operations  1.47 us (1%)
    all_to_all x3, starting transfers between devices, exchange(): return lax.all_to_all(value, 'dap', split_axis=0, concat_axis=0, tiled=True)  31.6 us
    all_to_all x3, waiting for transfers between devices, exchange(): return lax.all_to_all(value, 'dap', split_axis=0, concat_axis=0, tiled=True)  31 us
    all_to_all x1, blocking collectives, exchange(): return lax.all_to_all(value, 'dap', split_axis=0, concat_axis=0, tiled=True)  27.9 us
    pallas_call x6, Pallas kernels, apply(): pl.pallas_call(kernel, out_shape=outs, in_specs=[vmem] * len(operands), o...  19.5 us
    ppermute x3, waiting for transfers between devices, swap(): return lax.ppermute(value, 'dap', [(i, i ^ distance) for i in range(PEERS)])  11.2 us
    ppermute x3, starting transfers between devices, swap(): return lax.ppermute(value, 'dap', [(i, i ^ distance) for i in range(PEERS)])  8.12 us
  transfers between devices with their start and end apart: 6, of which 6 were waited for; matrix products, arithmetic and copies ran while one was open for 1% of the time, Pallas kernels for 0%

profile of v2, /device:TPU:1, one launch (start us, length us, event | category | flops | bytes accessed | tf_op | source)
XLA Modules:
  0.0 133.9 jit_solution(15628104225785982134)
XLA Ops:
  1.3 0.8 add_multiply_fusion
  2.1 0.1 copy.24.pen_ref
  2.3 1.4 %copy.23 = bf16[256,4,256]{0,2,1:T(8,128)(2,1)S(1)} copy(bf16[256,4,256]{2,1,0:T(4,128)(2,1)} %param.12) | data formatting | bytes 1048576 | tf_op args[2]
  3.7 3.9 %shard_map.153 = bf16[64,32,128]{2,1,0:T(8,128)(2,1)} custom-call(bf16[4,256,128]{2,1,0:T(8,128)(2,1)S(1)} %copy-done.1, bf16[4,256,128]{2,1,0:T(8,128)(2,1)S(1)} %copy-done.3, bf16[4,256,256]{2,1,0:T(8,128)(2,1)S(1)} %bitcast.11, f32[256,1]{1,0:T(8,128)S(1)} %copy.24.pen_ref, bf16[128,512]{1,0:T(8,128)(2,1)S(1)} %copy-done, bf16[128,128]{1,0:T(8,128)(2,1)S(1)} %copy-done.4), custom_call_target="tpu_custom_call" | custom-call | tf_op jit(solution)/shard_map/pallas_call | solution.py:328
  7.5 17.8 %all-to-all-start = ((bf16[64,32,128]{2,1,0:T(8,128)(2,1)}), bf16[64,32,128]{2,1,0:T(8,128)(2,1)S(1)}, u32[]{:S(2)}, u32[]{:S(2)}) async-start(bf16[64,32,128]{2,1,0:T(8,128)(2,1)} %shard_map.153), calls=%async_computation | async-start | bytes 1048576 | tf_op jit(solution)/shard_map/all_to_all | solution.py:345
  25.4 0.1 copy.26
  25.6 0.3 copy.25
  25.9 18.1 %all-to-all-done.recv_ref = bf16[64,32,128]{2,1,0:T(8,128)(2,1)S(1)} async-done(((bf16[64,32,128]{2,1,0:T(8,128)(2,1)}), bf16[64,32,128]{2,1,0:T(8,128)(2,1)S(1)}, u32[]{:S(2)}, u32[]{:S(2)}) %all-to-all-start) | async-done | bytes 524320 | tf_op jit(solution)/shard_map/all_to_all | solution.py:345
  44.0 6.8 %shard_map.154 = (bf16[64,16,128]{2,1,0:T(8,128)(2,1)}, bf16[1344,128]{1,0:T(8,128)(2,1)S(1)}, f32[1344,128]{1,0:T(8,128)S(1)}) custom-call(bf16[64,32,128]{2,1,0:T(8,128)(2,1)S(1)} %all-to-all-done.recv_ref, bf16[4,256,256]{2,1,0:T(8,128)(2,1)S(1)} %bitcast.13, f32[256,1]{1,0:T(8,128)S(1)} %copy.24.pen_ref, bf16[128,512]{1,0:T(8,128)(2,1)S(1)} %copy-done.2, ...), custom_call_target="tpu_custom_call" | custom-call | tf_op jit(solution)/shard_map/pallas_call | solution.py:328
  50.8 7.6 %all-to-all-start.1 = ((bf16[64,16,128]{2,1,0:T(8,128)(2,1)}), bf16[64,16,128]{2,1,0:T(8,128)(2,1)S(1)}, u32[]{:S(2)}, u32[]{:S(2)}) async-start(bf16[64,16,128]{2,1,0:T(8,128)(2,1)} %get-tuple-element.23), calls=%async_computation.1 | async-start | bytes 524288 | tf_op jit(solution)/shard_map/all_to_all | solution.py:345
  58.5 2.5 %collective-permute-start = (bf16[1344,128]{1,0:T(8,128)(2,1)S(1)}, bf16[1344,128]{1,0:T(8,128)(2,1)S(1)}, u32[]{:S(2)}, u32[]{:S(2)}) collective-permute-start(bf16[1344,128]{1,0:T(8,128)(2,1)S(1)} %get-tuple-element.25), channel_id=1, source_target_pairs={{0,1},{1,0},{2,3},{3,2},{4,5},{5,4},{6,7},{7,6},{8,9},{9,8},{10,11... | collective-permute-start | bytes 1032200 | tf_op jit(solution)/shard_map/ppermute | solution.py:349
  61.1 0.1 copy.29
  61.3 0.8 collective-permute-done.end_got_ref
  62.1 10.2 %all-to-all-done.1.recv_ref = bf16[64,16,128]{2,1,0:T(8,128)(2,1)S(1)} async-done(((bf16[64,16,128]{2,1,0:T(8,128)(2,1)}), bf16[64,16,128]{2,1,0:T(8,128)(2,1)S(1)}, u32[]{:S(2)}, u32[]{:S(2)}) %all-to-all-start.1) | async-done | bytes 262176 | tf_op jit(solution)/shard_map/all_to_all | solution.py:345
  72.3 7.1 %shard_map.155 = (bf16[4,256,128]{2,1,0:T(8,128)(2,1)}, bf16[64,32,128]{2,1,0:T(8,128)(2,1)}, bf16[1024,128]{1,0:T(8,128)(2,1)S(1)}, f32[1024,128]{1,0:T(8,128)S(1)}) custom-call(bf16[4,256,128]{2,1,0:T(8,128)(2,1)S(1)} %copy-done.1, bf16[64,16,128]{2,1,0:T(8,128)(2,1)S(1)} %all-to-all-done.1.recv_ref, bf16[4,256,256]{2,1,0:T(8,128)(2,1)S(1)} %bitcast.12, ...), custom_call_target="tpu_custom_call" | custom-call | tf_op jit(solution)/shard_map/pallas_call | solution.py:328
  79.5 6.2 %all-to-all-start.2 = ((bf16[64,32,128]{2,1,0:T(8,128)(2,1)}), bf16[64,32,128]{2,1,0:T(8,128)(2,1)S(1)}, u32[]{:S(2)}, u32[]{:S(2)}) async-start(bf16[64,32,128]{2,1,0:T(8,128)(2,1)} %get-tuple-element.27), calls=%async_computation.2 | async-start | bytes 1048576 | tf_op jit(solution)/shard_map/all_to_all | solution.py:345
  85.7 2.4 %collective-permute-start.1 = (bf16[1024,128]{1,0:T(8,128)(2,1)S(1)}, bf16[1024,128]{1,0:T(8,128)(2,1)S(1)}, u32[]{:S(2)}, u32[]{:S(2)}) collective-permute-start(bf16[1024,128]{1,0:T(8,128)(2,1)S(1)} %get-tuple-element.29), channel_id=1, source_target_pairs={{0,1},{1,0},{2,3},{3,2},{4,5},{5,4},{6,7},{7,6},{8,9},{9,8},{10,11... | collective-permute-start | bytes 786440 | tf_op jit(solution)/shard_map/ppermute | solution.py:349
  88.0 1.1 collective-permute-done.1.got_ref
  89.2 3.2 %collective-permute-start.2 = (bf16[512,128]{1,0:T(8,128)(2,1)S(1)}, bf16[512,128]{1,0:T(8,128)(2,1)S(1)}, u32[]{:S(2)}, u32[]{:S(2)}) collective-permute-start(bf16[512,128]{1,0:T(8,128)(2,1)S(1)} %get-tuple-element.31), channel_id=1, source_target_pairs={{0,2},{1,3},{2,0},{3,1},{4,6},{5,7},{6,4},{7,5},{8,10},{9,11},{10,... | collective-permute-start | bytes 393224 | tf_op jit(solution)/shard_map/ppermute | solution.py:349
  92.5 9.2 %collective-permute-done.2.got_ref = bf16[512,128]{1,0:T(8,128)(2,1)S(1)} collective-permute-done((bf16[512,128]{1,0:T(8,128)(2,1)S(1)}, bf16[512,128]{1,0:T(8,128)(2,1)S(1)}, u32[]{:S(2)}, u32[]{:S(2)}) %collective-permute-start.2) | collective-permute-done | bytes 131104 | tf_op jit(solution)/shard_map/ppermute | solution.py:349
  101.7 2.6 %all-to-all-done.2.recv_ref = bf16[64,32,128]{2,1,0:T(8,128)(2,1)S(1)} async-done(((bf16[64,32,128]{2,1,0:T(8,128)(2,1)}), bf16[64,32,128]{2,1,0:T(8,128)(2,1)S(1)}, u32[]{:S(2)}, u32[]{:S(2)}) %all-to-all-start.2) | async-done | bytes 524320 | tf_op jit(solution)/shard_map/all_to_all | solution.py:345
  104.3 0.7 shard_map.157
  105.0 27.9 %all_to_all.20.recv_ref = bf16[64,32,128]{2,1,0:T(8,128)(2,1)S(1)} all-to-all(bf16[64,32,128]{2,1,0:T(8,128)(2,1)S(1)} %get-tuple-element.32), channel_id=1, replica_groups=mesh['dp'=8,'dap'=64] {'dap'}, dimensions={0} | all-to-all | bytes 1048576 | tf_op jit(solution)/shard_map/all_to_all | solution.py:345
  132.9 1.0 shard_map.158
  (17 shorter events, 0.3 us)
Async XLA Ops:
  2.2 1.4 %copy-start = (bf16[128,512]{1,0:T(8,128)(2,1)S(1)}, bf16[128,512]{1,0:T(8,128)(2,1)}, u32[]{:S(2)}) copy-start(bf16[128,512]{1,0:T(8,128)(2,1)} %w_in_ref.5) | copy-start | bytes 393220
  2.2 1.4 %copy-start.1 = (bf16[4,256,128]{2,1,0:T(8,128)(2,1)S(1)}, bf16[4,256,128]{2,1,0:T(8,128)(2,1)}, u32[]{:S(2)}) copy-start(bf16[4,256,128]{2,1,0:T(8,128)(2,1)} %x_ref.3) | copy-start | bytes 786436
  2.2 1.4 %copy-start.3 = (bf16[4,256,128]{2,1,0:T(8,128)(2,1)S(1)}, bf16[4,256,128]{2,1,0:T(8,128)(2,1)}, u32[]{:S(2)}) copy-start(bf16[4,256,128]{2,1,0:T(8,128)(2,1)} %cot_ref.1) | copy-start | bytes 786436
  2.2 1.4 %copy-start.4 = (bf16[128,128]{1,0:T(8,128)(2,1)S(1)}, bf16[128,128]{1,0:T(8,128)(2,1)}, u32[]{:S(2)}) copy-start(bf16[128,128]{1,0:T(8,128)(2,1)} %w_out_ref.1) | copy-start | bytes 98308
  7.5 17.8 %copy-start.6 = (bf16[128,128]{1,0:T(8,128)(2,1)S(1)}, bf16[128,128]{1,0:T(8,128)(2,1)}, u32[]{:S(2)}) copy-start(bf16[128,128]{1,0:T(8,128)(2,1)} %param.17) | copy-start | bytes 98308
  7.5 17.9 %copy-start.2 = (bf16[128,512]{1,0:T(8,128)(2,1)S(1)}, bf16[128,512]{1,0:T(8,128)(2,1)}, u32[]{:S(2)}) copy-start(bf16[128,512]{1,0:T(8,128)(2,1)} %w_in_ref.4) | copy-start | bytes 393220
  7.5 18.0 %copy-start.5 = (bf16[256,4,256]{2,1,0:T(4,128)(2,1)S(1)}, bf16[256,4,256]{2,1,0:T(4,128)(2,1)}, u32[]{:S(2)}) copy-start(bf16[256,4,256]{2,1,0:T(4,128)(2,1)} %param.13) | copy-start | bytes 1572868
  7.5 36.5 %all-to-all-start = ((bf16[64,32,128]{2,1,0:T(8,128)(2,1)}), bf16[64,32,128]{2,1,0:T(8,128)(2,1)S(1)}, u32[]{:S(2)}, u32[]{:S(2)}) async-start(bf16[64,32,128]{2,1,0:T(8,128)(2,1)} %shard_map.153), calls=%async_computation | async-start | bytes 1048576 | tf_op jit(solution)/shard_map/all_to_all | solution.py:345
  50.8 21.5 %all-to-all-start.1 = ((bf16[64,16,128]{2,1,0:T(8,128)(2,1)}), bf16[64,16,128]{2,1,0:T(8,128)(2,1)S(1)}, u32[]{:S(2)}, u32[]{:S(2)}) async-start(bf16[64,16,128]{2,1,0:T(8,128)(2,1)} %get-tuple-element.23), calls=%async_computation.1 | async-start | bytes 524288 | tf_op jit(solution)/shard_map/all_to_all | solution.py:345
  58.5 3.6 %collective-permute-start = (bf16[1344,128]{1,0:T(8,128)(2,1)S(1)}, bf16[1344,128]{1,0:T(8,128)(2,1)S(1)}, u32[]{:S(2)}, u32[]{:S(2)}) collective-permute-start(bf16[1344,128]{1,0:T(8,128)(2,1)S(1)} %get-tuple-element.25), channel_id=1, source_target_pairs={{0,1},{1,0},{2,3},{3,2},{4,5},{5,4},{6,7},{7,6},{8,9},{9,8},{10,11... | collective-permute-start | bytes 1032200 | tf_op jit(solution)/shard_map/ppermute | solution.py:349
  79.5 24.8 %all-to-all-start.2 = ((bf16[64,32,128]{2,1,0:T(8,128)(2,1)}), bf16[64,32,128]{2,1,0:T(8,128)(2,1)S(1)}, u32[]{:S(2)}, u32[]{:S(2)}) async-start(bf16[64,32,128]{2,1,0:T(8,128)(2,1)} %get-tuple-element.27), calls=%async_computation.2 | async-start | bytes 1048576 | tf_op jit(solution)/shard_map/all_to_all | solution.py:345
  85.7 3.5 %collective-permute-start.1 = (bf16[1024,128]{1,0:T(8,128)(2,1)S(1)}, bf16[1024,128]{1,0:T(8,128)(2,1)S(1)}, u32[]{:S(2)}, u32[]{:S(2)}) collective-permute-start(bf16[1024,128]{1,0:T(8,128)(2,1)S(1)} %get-tuple-element.29), channel_id=1, source_target_pairs={{0,1},{1,0},{2,3},{3,2},{4,5},{5,4},{6,7},{7,6},{8,9},{9,8},{10,11... | collective-permute-start | bytes 786440 | tf_op jit(solution)/shard_map/ppermute | solution.py:349
  89.2 12.5 %collective-permute-start.2 = (bf16[512,128]{1,0:T(8,128)(2,1)S(1)}, bf16[512,128]{1,0:T(8,128)(2,1)S(1)}, u32[]{:S(2)}, u32[]{:S(2)}) collective-permute-start(bf16[512,128]{1,0:T(8,128)(2,1)S(1)} %get-tuple-element.31), channel_id=1, source_target_pairs={{0,2},{1,3},{2,0},{3,1},{4,6},{5,7},{6,4},{7,5},{8,10},{9,11},{10,... | collective-permute-start | bytes 393224 | tf_op jit(solution)/shard_map/ppermute | solution.py:349

commit v3 on v2

--- a/solution.py
+++ b/solution.py
@@ -11,6 +11,7 @@
 DH = 32
 N = 256
 C = 128
+CHAIN = 4096
 R = 4
 PEERS = N // R
 
@@ -20,7 +21,7 @@
 f32 = jnp.float32
 bf16 = jnp.bfloat16
 
-VMEM_LIMIT = 40 * 1024 * 1024
+VMEM_LIMIT = 20 * 1024 * 1024
 
 GROUP = 4
 
@@ -86,9 +87,36 @@
     return [jnp.concatenate(row, axis=0).T for row in parts]
 
 
-def start_forward_kernel(x_ref, cot_ref, bias_ref, pen_ref, w_in_ref, w_out_ref, send_ref, stage, first_packed, cot_packed):
+def window_penalty(mask_ref, offset_ref):
+    rows = CHAIN // C
+    offset = offset_ref[0]
+    first, shift = offset // C, offset % C
+    back = jnp.where(shift == 0, 0, C - shift)
+    lane = lax.broadcasted_iota(jnp.int32, (8, C), 1)
+    turned = []
+    for i in range(N // C + 1):
+        row = jnp.broadcast_to(mask_ref[pl.ds(jnp.minimum(first + i, rows - 1), 1), :], (8, C))
+        turned.append(pltpu.roll(row, back, 1))
+    columns = []
+    for i in range(N // C):
+        window = jnp.where(lane + shift < C, turned[i], turned[i + 1])
+        penalty = (window.astype(f32) - 1.0) * MASK_PENALTY
+        columns.append(jnp.broadcast_to(penalty[:1], (C, C)).T)
+    return jnp.concatenate(columns, axis=0)
+
+
+def wide_penalty(penalty):
+    return jnp.concatenate([penalty] * (N // C), axis=1)
+
+
+def start_forward_kernel(
+    x_ref, cot_ref, bias_ref, mask_ref, offset_ref, w_in_ref, w_out_ref,
+    send_ref, pen_ref, stage, first_packed, cot_packed,
+):
     masks = head_masks()
-    penalty = jnp.broadcast_to(pen_ref[...], (N, N))
+    column = window_penalty(mask_ref, offset_ref)
+    pen_ref[...] = column
+    penalty = wide_penalty(column)
     x = x_ref[...].reshape(R * N, C).astype(f32)
     normed, _ = layer_stats(x)
     queries, keys, values, gate = project(normed.astype(bf16), w_in_ref[...])
@@ -180,31 +208,30 @@
 WEIGHT_BLOCKS = 5
 BIAS_HALF = 2 * PEERS * CHUNKS
 WEIGHT_HALF = WEIGHT_BLOCKS * PEERS
-SEND_ROWS = 32
 WEIGHT_ROWS = 16
+TERM_ROWS = 2 * CHUNKS + WEIGHT_ROWS
+TOTAL_ROWS = WEIGHT_ROWS + CHUNKS
+
+
+CHIPS = PEERS // 2
 
 
 def core_index():
-    return lax.axis_index("dap") % 2
-
-
-def row_parity():
-    return (lax.axis_index("dap") // 2) % 2
-
-
-def split_bias(bias_sum, bias_packed, core):
+    return lax.axis_index("core")
+
+
+def bias_terms(bias_sum, bias_packed):
     eye = (lax.broadcasted_iota(jnp.int32, (N, N), 0) == lax.broadcasted_iota(jnp.int32, (N, N), 1)).astype(bf16)
     for h in range(H):
         by_query = nt(eye, bias_sum[h].astype(bf16))
         for half in range(N // C):
             bias_packed[pl.ds(half * H + h, N, stride=CHUNKS), :] = by_query[:, half * C : (half + 1) * C]
-    terms = bias_packed[...].reshape(PEERS, R, CHUNKS, C)
-    keep, give = [], []
-    for parity in range(2):
-        even, odd = terms[:, 2 * parity], terms[:, 2 * parity + 1]
-        keep.append(jnp.where(core == 0, even, odd).reshape(PEERS * CHUNKS, C))
-        give.append(jnp.where(core == 0, odd, even).reshape(PEERS * CHUNKS, C))
-    return keep, give
+    return bias_packed[...].reshape(PEERS, R, CHUNKS, C)
+
+
+def core_split(even, odd, core, keep_ref, give_ref, rows):
+    keep_ref[rows, :] = jnp.where(core == 0, even, odd)
+    give_ref[rows, :] = jnp.where(core == 0, odd, even).astype(bf16)
 
 
 def end_kernel(
@@ -214,7 +241,7 @@
 ):
     masks = head_masks()
     core = core_index()
-    penalty = jnp.broadcast_to(pen_ref[...], (N, N))
+    penalty = wide_penalty(pen_ref[...])
     x_all[...] = recv_ref[:, : R * R, :].astype(f32).reshape(N * R, C)
     up_all[...] = recv_ref[:, R * R :, :].astype(f32).reshape(N * R, C)
     for first in range(0, R, GROUP):
@@ -226,17 +253,13 @@
         for r, grad in zip(group, grads):
             pack_rows(grad, r, stage.at[r], grad_packed)
     send_ref[...] = grad_packed[...].reshape(PEERS, R * R, C).astype(bf16)
-    keep, give = split_bias(bias_sum, bias_packed, core)
+    terms = bias_terms(bias_sum, bias_packed)
     for parity in range(2):
-        rows = pl.ds(parity * PEERS * CHUNKS, PEERS * CHUNKS)
-        keep_ref[rows, :] = keep[parity]
-        give_ref[rows, :] = give[parity].astype(bf16)
+        even, odd = (terms[:, 2 * parity + i].reshape(PEERS * CHUNKS, C) for i in range(2))
+        core_split(even, odd, core, keep_ref, give_ref, pl.ds(parity * PEERS * CHUNKS, PEERS * CHUNKS))
     for q in range(WEIGHT_BLOCKS):
-        even = weight_sum.at[q][pl.ds(0, PEERS, stride=2), :]
-        odd = weight_sum.at[q][pl.ds(1, PEERS, stride=2), :]
-        rows = pl.ds(BIAS_HALF + q * PEERS, PEERS)
-        keep_ref[rows, :] = jnp.where(core == 0, even, odd)
-        give_ref[rows, :] = jnp.where(core == 0, odd, even).astype(bf16)
+        even, odd = (weight_sum.at[q][pl.ds(i, PEERS, stride=2), :] for i in range(2))
+        core_split(even, odd, core, keep_ref, give_ref, pl.ds(BIAS_HALF + q * PEERS, PEERS))
 
 
 def start_kernel(
@@ -246,7 +269,7 @@
 ):
     masks = head_masks()
     core = core_index()
-    penalty = jnp.broadcast_to(pen_ref[...], (N, N))
+    penalty = wide_penalty(pen_ref[...])
     up_all[...] = recv_ref[...].astype(f32).reshape(N * R, C)
     for first in range(0, R, GROUP):
         group = range(first, first + GROUP)
@@ -264,75 +287,74 @@
             weight_packed[pl.ds(q * 2 + parity, PEERS, stride=WEIGHT_ROWS), :] = block
         block = end_terms[BIAS_HALF + q * PEERS : BIAS_HALF + (q + 1) * PEERS]
         weight_packed[pl.ds(2 * WEIGHT_BLOCKS + q, PEERS, stride=WEIGHT_ROWS), :] = block
-    end_bias = [
-        end_terms[parity * PEERS * CHUNKS : (parity + 1) * PEERS * CHUNKS].reshape(PEERS, CHUNKS, C)
-        for parity in range(2)
-    ]
+    end_bias = by_parity(end_terms[:BIAS_HALF])
     weights = weight_packed[...].reshape(PEERS, WEIGHT_ROWS, C)
     send_ref[...] = jnp.concatenate(end_bias + [weights], axis=1).astype(bf16)
-    keep, give = split_bias(bias_sum, bias_packed, core)
+    terms = bias_terms(bias_sum, bias_packed).reshape(CHIPS, 2, R * CHUNKS, C)
+    even, odd = (terms[:, i].reshape(BIAS_HALF, C) for i in range(2))
+    core_split(even, odd, core, keep_ref, give_ref, slice(None))
+
+
+def by_parity(rows):
+    return [
+        rows[parity * PEERS * CHUNKS : (parity + 1) * PEERS * CHUNKS].reshape(PEERS, CHUNKS, C) for parity in range(2)
+    ]
+
+
+def write_bias(rows, residue, out_ref):
+    for half in range(N // C):
+        out_ref[residue, :, half * C : (half + 1) * C] = rows[half * H : (half + 1) * H]
+
+
+def middle_kernel(recv_ref, keep_ref, got_ref, send_ref, bias_ref):
+    by_core = jnp.sum(recv_ref[...].astype(f32).reshape(CHIPS, 2, TERM_ROWS, C), axis=0)
     for parity in range(2):
-        rows = pl.ds(parity * PEERS * CHUNKS, PEERS * CHUNKS)
-        keep_ref[rows, :] = keep[parity]
-        give_ref[rows, :] = give[parity].astype(bf16)
-
-
-def pair_sum_kernel(keep_ref, got_ref, next_keep_ref, next_give_ref):
-    total = keep_ref[...] + got_ref[...].astype(f32)
-    low, high = total[: PEERS * CHUNKS], total[PEERS * CHUNKS :]
-    parity = row_parity()
-    next_keep_ref[...] = jnp.where(parity == 0, low, high)
-    next_give_ref[...] = jnp.where(parity == 0, high, low).astype(bf16)
-
-
-def write_bias(rows, out_ref):
-    for residue in range(R):
-        for half in range(N // C):
-            out_ref[residue, :, half * C : (half + 1) * C] = rows[residue][half * H : (half + 1) * H]
-
-
-def middle_kernel(recv_ref, keep_ref, got_ref, bias_ref, send_ref):
-    by_core = jnp.sum(recv_ref[...].astype(f32).reshape(PEERS // 2, 2, SEND_ROWS, C), axis=0)
-    end_bias = [by_core[core, parity * CHUNKS : (parity + 1) * CHUNKS] for parity in range(2) for core in range(2)]
-    write_bias(end_bias, bias_ref)
+        for core in range(2):
+            write_bias(by_core[core, parity * CHUNKS : (parity + 1) * CHUNKS], 2 * parity + core, bias_ref)
     even, odd = by_core[0, 2 * CHUNKS :], by_core[1, 2 * CHUNKS :]
     slot = lax.broadcasted_iota(jnp.int32, (WEIGHT_ROWS, C), 0)
     totals = jnp.concatenate([even + jnp.where(slot < 2 * WEIGHT_BLOCKS, odd, 0.0), odd[CHUNKS:]], axis=0)
-    bias_terms = (keep_ref[...] + got_ref[...].astype(f32)).reshape(PEERS, CHUNKS, C)
-    everyone = jnp.broadcast_to(totals[None], (PEERS, SEND_ROWS - CHUNKS, C))
-    send_ref[...] = jnp.concatenate([bias_terms, everyone], axis=1).astype(bf16)
-
-
-def last_kernel(recv_ref, bias_ref, in_start, out_start, in_end, out_end, stage, block):
-    received = recv_ref[...].astype(f32)
-    write_bias(jnp.sum(received[:, :CHUNKS].reshape(PEERS // R, R, CHUNKS, C), axis=0), bias_ref)
-    span = SEND_ROWS - CHUNKS
-    stage[...] = received[:, CHUNKS:].reshape(PEERS * span, C) * (1.0 / N)
+    bias_rows = (keep_ref[...] + got_ref[...].astype(f32)).reshape(CHIPS, R * CHUNKS, C)
+    everyone = jnp.broadcast_to(totals[None], (CHIPS, TOTAL_ROWS, C))
+    send_ref[...] = jnp.concatenate([bias_rows, everyone], axis=1).astype(bf16)
+
+
+def totals_kernel(recv_ref, totals_ref):
+    totals_ref[...] = recv_ref[...].astype(f32)[:, R * CHUNKS :].astype(bf16)
+
+
+def last_kernel(recv_ref, totals_ref, bias_ref, in_start, out_start, in_end, out_end, stage, block):
+    bias = jnp.sum(recv_ref[...].astype(f32)[:, : R * CHUNKS], axis=0)
+    for residue in range(R):
+        write_bias(bias[residue * CHUNKS : (residue + 1) * CHUNKS], residue, bias_ref)
+    stage[...] = totals_ref[...].astype(f32).reshape(PEERS * TOTAL_ROWS, C) * (1.0 / N)
     end_slots = (2 * WEIGHT_BLOCKS, WEIGHT_ROWS + 2 * WEIGHT_BLOCKS - CHUNKS)
     for part, (win, wout) in enumerate(((in_start, out_start), (in_end, out_end))):
         for q in range(WEIGHT_BLOCKS):
-            for parity in range(2):
-                row = q * 2 + parity if part == 0 else end_slots[parity] + q
-                block[pl.ds(parity, PEERS, stride=2), :] = stage[pl.ds(row, PEERS, stride=span), :]
+            for core in range(2):
+                for parity in range(2):
+                    row = q * 2 + parity if part == 0 else end_slots[parity] + q
+                    value = stage[pl.ds(core * CHIPS * TOTAL_ROWS + row, CHIPS, stride=TOTAL_ROWS), :]
+                    block[pl.ds(2 * core + parity, CHIPS, stride=4), :] = value
             if q < 4:
                 win[:, q * C : (q + 1) * C] = block[...]
             else:
                 wout[...] = block[...]
 
 
-def call(kernel, outs, scratch=(), far=()):
+def call(kernel, outs, scratch=(), places=None):
     vmem = pl.BlockSpec(memory_space=pltpu.VMEM)
+    places = places or {}
 
     def apply(*operands):
-        placed = [pltpu.with_memory_space_constraint(v, pltpu.HBM) if i in far else v for i, v in enumerate(operands)]
         return pl.pallas_call(
             kernel,
             out_shape=outs,
-            in_specs=[vmem] * len(operands),
+            in_specs=[pl.BlockSpec(memory_space=places[i]) if i in places else vmem for i in range(len(operands))],
             out_specs=jax.tree.map(lambda _: vmem, outs),
             scratch_shapes=list(scratch),
             compiler_params=pltpu.CompilerParams(vmem_limit_bytes=VMEM_LIMIT),
-        )(*placed)
+        )(*operands)
 
     return apply
 
@@ -341,12 +363,13 @@
     return jax.ShapeDtypeStruct(shape, dtype)
 
 
-def exchange(value):
-    return lax.all_to_all(value, "dap", split_axis=0, concat_axis=0, tiled=True)
-
-
-def swap(value, distance):
-    return lax.ppermute(value, "dap", [(i, i ^ distance) for i in range(PEERS)])
+def exchange(value, axes=("chip", "core")):
+    rows = value.reshape(-1, C)
+    return lax.all_to_all(rows, axes, split_axis=0, concat_axis=0, tiled=True).reshape(value.shape)
+
+
+def swap(value):
+    return lax.ppermute(value, "core", [(0, 1), (1, 0)])
 
 
 def shards(
@@ -361,8 +384,6 @@
     residue_mask,
     window_offset,
 ):
-    window = lax.dynamic_slice_in_dim(residue_mask, window_offset[0], N)
-    penalty = ((window.astype(f32) - 1.0) * MASK_PENALTY)[:, None]
     bias_start_t = jnp.transpose(bias_start, (1, 2, 0))
     bias_end_t = jnp.transpose(bias_end, (1, 2, 0))
     rows_f32 = pltpu.VMEM((N * R, C), f32)
@@ -372,9 +393,12 @@
     weight_packed = pltpu.VMEM((PEERS * WEIGHT_ROWS, C), f32)
     term_rows = PEERS * CHUNKS
 
-    send = call(start_forward_kernel, struct((PEERS, 2 * R * R, C), bf16), (pltpu.VMEM((2 * R, N, C), f32), rows_f32, rows_f32))(
-        pair_act, cotangent, bias_start_t, penalty, w_in_start, w_out_start
-    )
+    send, penalty = call(
+        start_forward_kernel,
+        (struct((PEERS, 2 * R * R, C), bf16), struct((N, C), f32)),
+        (pltpu.VMEM((2 * R, N, C), f32), rows_f32, rows_f32),
+        {4: pltpu.SMEM},
+    )(pair_act, cotangent, bias_start_t, residue_mask.reshape(CHAIN // C, C), window_offset, w_in_start, w_out_start)
     recv = exchange(send)
     grad_send, end_give, end_keep = call(
         end_kernel,
@@ -386,40 +410,42 @@
         (rows_f32, rows_f32, pltpu.VMEM((R, N, C), f32), rows_f32, bias_sum, weight_sum, bias_packed),
     )(recv, bias_end_t, penalty, w_in_end, w_in_end.T, w_out_end.T)
     grad_recv = exchange(grad_send)
-    end_got = swap(end_give, 1)
+    end_got = swap(end_give)
     grad_pair, term_send, start_give, start_keep = call(
         start_kernel,
         (
             struct((R, N, C), bf16),
-            struct((PEERS, SEND_ROWS, C), bf16),
+            struct((PEERS, TERM_ROWS, C), bf16),
             struct((BIAS_HALF, C), bf16),
             struct((BIAS_HALF, C), f32),
         ),
         (rows_f32, bias_sum, weight_sum, bias_packed, weight_packed),
     )(pair_act, grad_recv, bias_start_t, penalty, w_in_start, w_in_start.T, w_out_start.T, end_keep, end_got)
     term_recv = exchange(term_send)
-    pair_keep, pair_give = call(pair_sum_kernel, (struct((term_rows, C), f32), struct((term_rows, C), bf16)))(
-        start_keep, swap(start_give, 1)
-    )
-    pair_got = swap(pair_give, 2)
-    grad_bias_end, last_send = call(
-        middle_kernel, (struct((R, H, N), f32), struct((PEERS, SEND_ROWS, C), bf16))
-    )(term_recv, pair_keep, pair_got)
-    last_recv = exchange(last_send)
+    start_got = swap(start_give)
+    last_rows = R * CHUNKS + TOTAL_ROWS
+    last_send, grad_bias_end = call(
+        middle_kernel, (struct((CHIPS, last_rows, C), bf16), struct((R, H, N), f32))
+    )(term_recv, start_keep, start_got)
+    last_recv = exchange(last_send, "chip")
+    totals = call(totals_kernel, struct((CHIPS, TOTAL_ROWS, C), bf16))(last_recv)
+    totals = lax.all_gather(totals, "core", axis=0, tiled=True)
     grad_bias_start, *weights = call(
         last_kernel,
         (struct((R, H, N), f32),) + tuple(struct(shape, f32) for shape in ((C, 4 * C), (C, C), (C, 4 * C), (C, C))),
-        (pltpu.VMEM((PEERS * (SEND_ROWS - CHUNKS), C), f32), pltpu.VMEM((C, C), f32)),
-    )(last_recv)
+        (pltpu.VMEM((PEERS * TOTAL_ROWS, C), f32), pltpu.VMEM((C, C), f32)),
+    )(last_recv, totals)
     return (grad_pair, grad_bias_start, grad_bias_end, *weights)
 
 
 def solution(mesh):
-    rows = P(("dp", "dap"), None, None)
+    dp, dap = mesh.devices.shape
+    fine = jax.sharding.Mesh(mesh.devices.reshape(dp, dap // 2, 2), ("dp", "chip", "core"))
+    rows = P(("dp", "chip", "core"), None, None)
     placed = (rows, rows, P("dp", None, None), P("dp", None, None), P(), P(), P(), P(), P("dp"), P("dp"))
     return jax.shard_map(
         shards,
-        mesh=mesh,
+        mesh=fine,
         in_specs=placed,
         out_specs=(rows, rows, rows, P("dp", None), P("dp", None), P("dp", None), P("dp", None)),
         check_vma=False,

time: 134 us -> 132 us (0.985)
  starting transfers between devices: 39.7 us -> 36.5 us
  waiting for transfers between devices: 42.2 us -> 45.4 us
  blocking collectives: 27.9 us -> 26.4 us
    all_to_all x3, waiting for transfers between devices: 31 us -> 43.5 us  [exchange(): lax.all_to_all(rows, axes, split_axis=0, concat_axis=0, tiled=True)]
    ppermute x3 -> x2, waiting for transfers between devices: 11.2 us -> 1.97 us  [swap(): return lax.ppermute(value, 'core', [(0, 1), (1, 0)])]
    all_to_all x1, blocking collectives: 27.9 us -> 20.6 us  [exchange(): lax.all_to_all(rows, axes, split_axis=0, concat_axis=0, tiled=True)]
    all_gather x0 -> x1, blocking collectives: none -> 5.82 us  [shards(): totals = lax.all_gather(totals, 'core', axis=0, tiled=True)]
    ppermute x3 -> x2, starting transfers between devices: 8.12 us -> 4.91 us  [swap(): return lax.ppermute(value, 'core', [(0, 1), (1, 0)])]
  transfers between devices with their start and end apart: 6 -> 5, of which waited for: 6 -> 5; matrix products, arithmetic and copies ran while one was open for 1% -> 1% of each run, Pallas kernels for 0% -> 0%
where the time goes in v3:
time: 132 us; the launch traced here: 131 us
  waiting for transfers between devices  45.4 us (34%)
  starting transfers between devices  36.5 us (28%)
  blocking collectives  26.4 us (20%)
  Pallas kernels  19.4 us (15%)
  local copies, waits for them, and re-layouts  2.21 us (2%)
  between operations  1.47 us (1%)
    all_to_all x3, waiting for transfers between devices, exchange(): lax.all_to_all(rows, axes, split_axis=0, concat_axis=0, tiled=True)  43.5 us
    all_to_all x3, starting transfers between devices, exchange(): lax.all_to_all(rows, axes, split_axis=0, concat_axis=0, tiled=True)  31.6 us
    all_to_all x1, blocking collectives, exchange(): lax.all_to_all(rows, axes, split_axis=0, concat_axis=0, tiled=True)  20.6 us
    pallas_call x6, Pallas kernels, apply(): pl.pallas_call(kernel, out_shape=outs, in_specs=[pl.BlockSpec(memory_spac...  19.4 us
    all_gather x1, blocking collectives, shards(): totals = lax.all_gather(totals, 'core', axis=0, tiled=True)  5.82 us
    ppermute x2, starting transfers between devices, swap(): return lax.ppermute(value, 'core', [(0, 1), (1, 0)])  4.91 us
  transfers between devices with their start and end apart: 5, of which 5 were waited for; matrix products, arithmetic and copies ran while one was open for 1% of the time, Pallas kernels for 0%

profile of v3, /device:TPU:1, one launch (start us, length us, event | category | flops | bytes accessed | tf_op | source)
XLA Modules:
  0.0 131.4 jit_solution(12657025108983817784)
XLA Ops:
  1.3 1.4 %copy.23 = bf16[256,4,256]{0,2,1:T(8,128)(2,1)S(1)} copy(bf16[256,4,256]{2,1,0:T(4,128)(2,1)} %param.12) | data formatting | bytes 1048576 | tf_op args[2]
  2.8 3.8 %shard_map.153 = (bf16[64,32,128]{2,1,0:T(8,128)(2,1)}, f32[256,128]{1,0:T(8,128)S(1)}) custom-call(bf16[4,256,128]{2,1,0:T(8,128)(2,1)S(1)} %copy-done.1, bf16[4,256,128]{2,1,0:T(8,128)(2,1)S(1)} %copy-done.3, bf16[4,256,256]{2,1,0:T(8,128)(2,1)S(1)} %bitcast.7, s32[32,128]{1,0:T(8,128)S(1)} %bitcast.14, s32[1]{0:T(128)S(6)} %copy.29.offset_ref, ...), custom_call_target="tpu_custom_call" | custom-call | tf_op jit(solution)/shard_map/pallas_call | solution.py:350
  6.6 17.8 %all-to-all-start = ((bf16[64,32,128]{2,1,0:T(8,128)(2,1)}), bf16[64,32,128]{2,1,0:T(8,128)(2,1)S(1)}, u32[]{:S(2)}, u32[]{:S(2)}) async-start(bf16[64,32,128]{2,1,0:T(8,128)(2,1)} %get-tuple-element.23), calls=%async_computation | async-start | bytes 1048576 | tf_op jit(solution)/shard_map/all_to_all | solution.py:368
  24.4 0.1 copy.26
  24.5 0.1 copy.25
  24.6 0.0 copy-done.6
  24.6 0.3 copy.24
  25.0 18.1 %all-to-all-done.recv_ref = bf16[64,32,128]{2,1,0:T(8,128)(2,1)S(1)} async-done(((bf16[64,32,128]{2,1,0:T(8,128)(2,1)}), bf16[64,32,128]{2,1,0:T(8,128)(2,1)S(1)}, u32[]{:S(2)}, u32[]{:S(2)}) %all-to-all-start) | async-done | bytes 524320 | tf_op jit(solution)/shard_map/all_to_all | solution.py:368
  43.1 6.8 %shard_map.154 = (bf16[64,16,128]{2,1,0:T(8,128)(2,1)}, bf16[1344,128]{1,0:T(8,128)(2,1)S(1)}, f32[1344,128]{1,0:T(8,128)S(1)}) custom-call(bf16[64,32,128]{2,1,0:T(8,128)(2,1)S(1)} %all-to-all-done.recv_ref, bf16[4,256,256]{2,1,0:T(8,128)(2,1)S(1)} %bitcast.9, f32[256,128]{1,0:T(8,128)S(1)} %get-tuple-element.24.pen_ref, bf16[128,512]{1,0:T(8,128)(2,1)S(1)} %copy-done.2, ...), custom_call_target="tpu_custom_call" | custom-call | tf_op jit(solution)/shard_map/pallas_call | solution.py:350
  49.9 7.7 %all-to-all-start.1 = ((bf16[64,16,128]{2,1,0:T(8,128)(2,1)}), bf16[64,16,128]{2,1,0:T(8,128)(2,1)S(1)}, u32[]{:S(2)}, u32[]{:S(2)}) async-start(bf16[64,16,128]{2,1,0:T(8,128)(2,1)} %get-tuple-element.25), calls=%async_computation.1 | async-start | bytes 524288 | tf_op jit(solution)/shard_map/all_to_all | solution.py:368
  57.6 2.5 %collective-permute-start = (bf16[1344,128]{1,0:T(8,128)(2,1)S(1)}, bf16[1344,128]{1,0:T(8,128)(2,1)S(1)}, u32[]{:S(2)}, u32[]{:S(2)}) collective-permute-start(bf16[1344,128]{1,0:T(8,128)(2,1)S(1)} %get-tuple-element.27), channel_id=1, source_target_pairs={{0,1},{1,0},{2,3},{3,2},{4,5},{5,4},{6,7},{7,6},{8,9},{9,8},{10,11... | collective-permute-start | bytes 1032200 | tf_op jit(solution)/shard_map/ppermute | solution.py:372
  60.1 0.1 copy.28
  60.2 0.1 copy.27
  60.4 0.8 collective-permute-done.end_got_ref
  61.2 10.2 %all-to-all-done.1.recv_ref = bf16[64,16,128]{2,1,0:T(8,128)(2,1)S(1)} async-done(((bf16[64,16,128]{2,1,0:T(8,128)(2,1)}), bf16[64,16,128]{2,1,0:T(8,128)(2,1)S(1)}, u32[]{:S(2)}, u32[]{:S(2)}) %all-to-all-start.1) | async-done | bytes 262176 | tf_op jit(solution)/shard_map/all_to_all | solution.py:368
  71.4 7.1 %shard_map.155 = (bf16[4,256,128]{2,1,0:T(8,128)(2,1)}, bf16[64,32,128]{2,1,0:T(8,128)(2,1)}, bf16[1024,128]{1,0:T(8,128)(2,1)S(1)}, f32[1024,128]{1,0:T(8,128)S(1)}) custom-call(bf16[4,256,128]{2,1,0:T(8,128)(2,1)S(1)} %copy-done.1, bf16[64,16,128]{2,1,0:T(8,128)(2,1)S(1)} %all-to-all-done.1.recv_ref, bf16[4,256,256]{2,1,0:T(8,128)(2,1)S(1)} %bitcast.8, ...), custom_call_target="tpu_custom_call" | custom-call | tf_op jit(solution)/shard_map/pallas_call | solution.py:350
  78.5 6.2 %all-to-all-start.2 = ((bf16[64,32,128]{2,1,0:T(8,128)(2,1)}), bf16[64,32,128]{2,1,0:T(8,128)(2,1)S(1)}, u32[]{:S(2)}, u32[]{:S(2)}) async-start(bf16[64,32,128]{2,1,0:T(8,128)(2,1)} %get-tuple-element.29), calls=%async_computation.2 | async-start | bytes 1048576 | tf_op jit(solution)/shard_map/all_to_all | solution.py:368
  84.7 2.4 %collective-permute-start.1 = (bf16[1024,128]{1,0:T(8,128)(2,1)S(1)}, bf16[1024,128]{1,0:T(8,128)(2,1)S(1)}, u32[]{:S(2)}, u32[]{:S(2)}) collective-permute-start(bf16[1024,128]{1,0:T(8,128)(2,1)S(1)} %get-tuple-element.31), channel_id=1, source_target_pairs={{0,1},{1,0},{2,3},{3,2},{4,5},{5,4},{6,7},{7,6},{8,9},{9,8},{10,11... | collective-permute-start | bytes 786440 | tf_op jit(solution)/shard_map/ppermute | solution.py:372
  87.1 1.1 collective-permute-done.1.got_ref
  88.2 15.1 %all-to-all-done.2.recv_ref = bf16[64,32,128]{2,1,0:T(8,128)(2,1)S(1)} async-done(((bf16[64,32,128]{2,1,0:T(8,128)(2,1)}), bf16[64,32,128]{2,1,0:T(8,128)(2,1)S(1)}, u32[]{:S(2)}, u32[]{:S(2)}) %all-to-all-start.2) | async-done | bytes 524320 | tf_op jit(solution)/shard_map/all_to_all | solution.py:368
  103.4 0.7 shard_map.156
  104.0 20.6 %all_to_all.24.recv_ref = bf16[32,56,128]{2,1,0:T(8,128)(2,1)S(1)} all-to-all(bf16[32,56,128]{2,1,0:T(8,128)(2,1)S(1)} %get-tuple-element.32), channel_id=1, replica_groups=mesh['dp'=8,'chip'=32,'core'=2] {'chip'}, dimensions={0} | all-to-all | bytes 917504 | tf_op jit(solution)/shard_map/all_to_all | solution.py:368
  124.6 5.8 %all_gather.3.totals_ref = bf16[64,24,128]{2,1,0:T(8,128)(2,1)S(1)} all-gather(bf16[32,24,128]{2,1,0:T(8,128)(2,1)S(1)} %shard_map.157), channel_id=1, replica_groups=mesh['dp'=8,'chip'=32,'core'=2] {'core'}, dimensions={0}, use_global_device_ids=true | all-gather | bytes 589824 | tf_op jit(solution)/shard_map/all_gather | solution.py:432
  130.5 1.0 shard_map.158
  (16 shorter events, 0.1 us)
Async XLA Ops:
  1.3 1.4 %copy-start = (bf16[128,512]{1,0:T(8,128)(2,1)S(1)}, bf16[128,512]{1,0:T(8,128)(2,1)}, u32[]{:S(2)}) copy-start(bf16[128,512]{1,0:T(8,128)(2,1)} %w_in_ref.5) | copy-start | bytes 393220
  1.3 1.4 %copy-start.1 = (bf16[4,256,128]{2,1,0:T(8,128)(2,1)S(1)}, bf16[4,256,128]{2,1,0:T(8,128)(2,1)}, u32[]{:S(2)}) copy-start(bf16[4,256,128]{2,1,0:T(8,128)(2,1)} %x_ref.3) | copy-start | bytes 786436
  1.3 1.4 %copy-start.3 = (bf16[4,256,128]{2,1,0:T(8,128)(2,1)S(1)}, bf16[4,256,128]{2,1,0:T(8,128)(2,1)}, u32[]{:S(2)}) copy-start(bf16[4,256,128]{2,1,0:T(8,128)(2,1)} %cot_ref.1) | copy-start | bytes 786436
  1.3 1.4 %copy-start.4 = (bf16[128,128]{1,0:T(8,128)(2,1)S(1)}, bf16[128,128]{1,0:T(8,128)(2,1)}, u32[]{:S(2)}) copy-start(bf16[128,128]{1,0:T(8,128)(2,1)} %w_out_ref.1) | copy-start | bytes 98308
  1.3 1.4 %copy-start.5 = (s32[4096]{0:T(1024)S(1)}, s32[4096]{0:T(1024)}, u32[]{:S(2)}) copy-start(s32[4096]{0:T(1024)} %param.18) | copy-start | bytes 49156
  6.6 17.8 %copy-start.7 = (bf16[128,128]{1,0:T(8,128)(2,1)S(1)}, bf16[128,128]{1,0:T(8,128)(2,1)}, u32[]{:S(2)}) copy-start(bf16[128,128]{1,0:T(8,128)(2,1)} %param.17) | copy-start | bytes 98308
  6.6 17.9 %copy-start.2 = (bf16[128,512]{1,0:T(8,128)(2,1)S(1)}, bf16[128,512]{1,0:T(8,128)(2,1)}, u32[]{:S(2)}) copy-start(bf16[128,512]{1,0:T(8,128)(2,1)} %w_in_ref.4) | copy-start | bytes 393220
  6.6 18.0 %copy-start.6 = (bf16[256,4,256]{2,1,0:T(4,128)(2,1)S(1)}, bf16[256,4,256]{2,1,0:T(4,128)(2,1)}, u32[]{:S(2)}) copy-start(bf16[256,4,256]{2,1,0:T(4,128)(2,1)} %param.13) | copy-start | bytes 1572868
  6.6 36.5 %all-to-all-start = ((bf16[64,32,128]{2,1,0:T(8,128)(2,1)}), bf16[64,32,128]{2,1,0:T(8,128)(2,1)S(1)}, u32[]{:S(2)}, u32[]{:S(2)}) async-start(bf16[64,32,128]{2,1,0:T(8,128)(2,1)} %get-tuple-element.23), calls=%async_computation | async-start | bytes 1048576 | tf_op jit(solution)/shard_map/all_to_all | solution.py:368
  49.9 21.5 %all-to-all-start.1 = ((bf16[64,16,128]{2,1,0:T(8,128)(2,1)}), bf16[64,16,128]{2,1,0:T(8,128)(2,1)S(1)}, u32[]{:S(2)}, u32[]{:S(2)}) async-start(bf16[64,16,128]{2,1,0:T(8,128)(2,1)} %get-tuple-element.25), calls=%async_computation.1 | async-start | bytes 524288 | tf_op jit(solution)/shard_map/all_to_all | solution.py:368
  57.6 3.6 %collective-permute-start = (bf16[1344,128]{1,0:T(8,128)(2,1)S(1)}, bf16[1344,128]{1,0:T(8,128)(2,1)S(1)}, u32[]{:S(2)}, u32[]{:S(2)}) collective-permute-start(bf16[1344,128]{1,0:T(8,128)(2,1)S(1)} %get-tuple-element.27), channel_id=1, source_target_pairs={{0,1},{1,0},{2,3},{3,2},{4,5},{5,4},{6,7},{7,6},{8,9},{9,8},{10,11... | collective-permute-start | bytes 1032200 | tf_op jit(solution)/shard_map/ppermute | solution.py:372
  78.5 24.8 %all-to-all-start.2 = ((bf16[64,32,128]{2,1,0:T(8,128)(2,1)}), bf16[64,32,128]{2,1,0:T(8,128)(2,1)S(1)}, u32[]{:S(2)}, u32[]{:S(2)}) async-start(bf16[64,32,128]{2,1,0:T(8,128)(2,1)} %get-tuple-element.29), calls=%async_computation.2 | async-start | bytes 1048576 | tf_op jit(solution)/shard_map/all_to_all | solution.py:368
  84.7 3.5 %collective-permute-start.1 = (bf16[1024,128]{1,0:T(8,128)(2,1)S(1)}, bf16[1024,128]{1,0:T(8,128)(2,1)S(1)}, u32[]{:S(2)}, u32[]{:S(2)}) collective-permute-start(bf16[1024,128]{1,0:T(8,128)(2,1)S(1)} %get-tuple-element.31), channel_id=1, source_target_pairs={{0,1},{1,0},{2,3},{3,2},{4,5},{5,4},{6,7},{7,6},{8,9},{9,8},{10,11... | collective-permute-start | bytes 786440 | tf_op jit(solution)/shard_map/ppermute | solution.py:372

commit v4 on v3

--- a/solution.py
+++ b/solution.py
@@ -70,14 +70,21 @@
 
 
 def softmax_all(keys_h, queries, bias_ref, penalty):
-    scores = [[nt(keys_h[r][h], queries[r]) for h in range(H)] for r in range(len(queries))]
+    scores = []
+    for r in range(len(queries)):
+        both = nt(jnp.concatenate(keys_h[r], axis=0), queries[r])
+        scores.append([both[h * N : (h + 1) * N] for h in range(H)])
     return [[head_softmax(row[h], bias_ref[h], penalty) for h in range(H)] for row in scores]
 
 
 def head_softmax(scores, bias_h, penalty):
-    scores = scores + bias_h.astype(f32) + penalty
-    exponent = jnp.exp(scores - jnp.max(scores, axis=0, keepdims=True))
-    return exponent * (1.0 / jnp.sum(exponent, axis=0, keepdims=True))
+    parts = []
+    for first in range(0, N, 128):
+        at = slice(first, first + 128)
+        block = scores[:, at] + bias_h[:, at].astype(f32) + penalty[:, at]
+        exponent = jnp.exp(block - jnp.max(block, axis=0, keepdims=True))
+        parts.append(exponent * (1.0 / jnp.sum(exponent, axis=0, keepdims=True)))
+    return jnp.concatenate(parts, axis=1)
 
 
 def attend_all(values_t, probs_b):
@@ -161,23 +168,33 @@
     gated = [(gate[r] * attended[r]).astype(bf16) for r in range(count)]
     grad_gate = [grad_gated[r] * attended[r] * gate[r] * (1.0 - gate[r]) for r in range(count)]
     grad_mixed = [(grad_gated[r] * gate[r]).astype(bf16) for r in range(count)]
-    grad_probs = [[nt(values_h[r][h], grad_mixed[r]) for h in range(H)] for r in range(count)]
+    grad_probs = []
+    for r in range(count):
+        both = nt(jnp.concatenate(values_h[r], axis=0), grad_mixed[r])
+        grad_probs.append([both[h * N : (h + 1) * N] for h in range(H)])
     scores_b = [[None] * H for _ in range(count)]
-    for h in range(H):
-        total = None
-        for r in range(count):
-            inner = jnp.sum(probs[r][h] * grad_probs[r][h], axis=0, keepdims=True)
-            grad_scores = probs[r][h] * (grad_probs[r][h] - inner)
-            scores_b[r][h] = grad_scores.astype(bf16)
-            total = grad_scores if total is None else total + grad_scores
-        if first:
-            bias_sum[h] = total
-        else:
-            bias_sum[h] += total
+    by_value = [[None] * H for _ in range(count)]
+    by_key = [[None] * H for _ in range(count)]
+    by_query = [[None] * H for _ in range(count)]
+    for step in range(H + 2):
+        if step < H:
+            h, total = step, None
+            for r in range(count):
+                inner = jnp.sum(probs[r][h] * grad_probs[r][h], axis=0, keepdims=True)
+                grad_scores = probs[r][h] * (grad_probs[r][h] - inner)
+                scores_b[r][h] = grad_scores.astype(bf16)
+                total = grad_scores if total is None else total + grad_scores
+                by_value[r][h] = nn(probs[r][h].astype(bf16), grad_mixed[r])
+            if first:
+                bias_sum[h] = total
+            else:
+                bias_sum[h] += total
+        if step >= 2:
+            h = step - 2
+            for r in range(count):
+                by_key[r][h] = nn(scores_b[r][h], queries[r])
+                by_query[r][h] = nn(keys_t[r][h * DH : (h + 1) * DH], scores_b[r][h])
     wins, wouts, grads = [], [], []
-    by_value = [[nn(probs[r][h].astype(bf16), grad_mixed[r]) for h in range(H)] for r in range(count)]
-    by_key = [[nn(scores_b[r][h], queries[r]) for h in range(H)] for r in range(count)]
-    by_query = [[nn(keys_t[r][h * DH : (h + 1) * DH], scores_b[r][h]) for h in range(H)] for r in range(count)]
     for r in range(count):
         grad_value, grad_key = by_value[r][0], by_key[r][0]
         for h in range(1, H):

time: 132 us -> 131 us (level)
  no operation moved by 1% of the time
where the time goes in v4:
time: 131 us
  waiting for transfers between devices  45.4 us (35%)
  starting transfers between devices  36.5 us (28%)
  blocking collectives  26.4 us (20%)
  Pallas kernels  18.9 us (14%)
  local copies, waits for them, and re-layouts  2.21 us (2%)
  between operations  1.47 us (1%)
    all_to_all x3, waiting for transfers between devices, exchange(): lax.all_to_all(rows, axes, split_axis=0, concat_axis=0, tiled=True)  43.5 us
    all_to_all x3, starting transfers between devices, exchange(): lax.all_to_all(rows, axes, split_axis=0, concat_axis=0, tiled=True)  31.6 us
    all_to_all x1, blocking collectives, exchange(): lax.all_to_all(rows, axes, split_axis=0, concat_axis=0, tiled=True)  20.6 us
    pallas_call x6, Pallas kernels, apply(): pl.pallas_call(kernel, out_shape=outs, in_specs=[pl.BlockSpec(memory_spac...  18.9 us
    all_gather x1, blocking collectives, shards(): totals = lax.all_gather(totals, 'core', axis=0, tiled=True)  5.82 us
    ppermute x2, starting transfers between devices, swap(): return lax.ppermute(value, 'core', [(0, 1), (1, 0)])  4.91 us
  transfers between devices with their start and end apart: 5, of which 5 were waited for; matrix products, arithmetic and copies ran while one was open for 1% of the time, Pallas kernels for 0%

profile of v4, /device:TPU:1, one launch (start us, length us, event | category | flops | bytes accessed | tf_op | source)
XLA Modules:
  0.0 130.9 jit_solution(17078596691928069302)
XLA Ops:
  1.3 1.4 %copy.23 = bf16[256,4,256]{0,2,1:T(8,128)(2,1)S(1)} copy(bf16[256,4,256]{2,1,0:T(4,128)(2,1)} %param.12) | data formatting | bytes 1048576 | tf_op args[2]
  2.8 3.8 %shard_map.153 = (bf16[64,32,128]{2,1,0:T(8,128)(2,1)}, f32[256,128]{1,0:T(8,128)S(1)}) custom-call(bf16[4,256,128]{2,1,0:T(8,128)(2,1)S(1)} %copy-done.1, bf16[4,256,128]{2,1,0:T(8,128)(2,1)S(1)} %copy-done.3, bf16[4,256,256]{2,1,0:T(8,128)(2,1)S(1)} %bitcast.7, s32[32,128]{1,0:T(8,128)S(1)} %bitcast.14, s32[1]{0:T(128)S(6)} %copy.29.offset_ref, ...), custom_call_target="tpu_custom_call" | custom-call | tf_op jit(solution)/shard_map/pallas_call | solution.py:367
  6.6 17.8 %all-to-all-start = ((bf16[64,32,128]{2,1,0:T(8,128)(2,1)}), bf16[64,32,128]{2,1,0:T(8,128)(2,1)S(1)}, u32[]{:S(2)}, u32[]{:S(2)}) async-start(bf16[64,32,128]{2,1,0:T(8,128)(2,1)} %get-tuple-element.23), calls=%async_computation | async-start | bytes 1048576 | tf_op jit(solution)/shard_map/all_to_all | solution.py:385
  24.4 0.1 copy.26
  24.5 0.0 copy-done.2
  24.5 0.1 copy.25
  24.6 0.3 copy.24
  25.0 18.1 %all-to-all-done.recv_ref = bf16[64,32,128]{2,1,0:T(8,128)(2,1)S(1)} async-done(((bf16[64,32,128]{2,1,0:T(8,128)(2,1)}), bf16[64,32,128]{2,1,0:T(8,128)(2,1)S(1)}, u32[]{:S(2)}, u32[]{:S(2)}) %all-to-all-start) | async-done | bytes 524320 | tf_op jit(solution)/shard_map/all_to_all | solution.py:385
  43.1 6.5 %shard_map.154 = (bf16[64,16,128]{2,1,0:T(8,128)(2,1)}, bf16[1344,128]{1,0:T(8,128)(2,1)S(1)}, f32[1344,128]{1,0:T(8,128)S(1)}) custom-call(bf16[64,32,128]{2,1,0:T(8,128)(2,1)S(1)} %all-to-all-done.recv_ref, bf16[4,256,256]{2,1,0:T(8,128)(2,1)S(1)} %bitcast.9, f32[256,128]{1,0:T(8,128)S(1)} %get-tuple-element.24.pen_ref, bf16[128,512]{1,0:T(8,128)(2,1)S(1)} %copy-done.2, ...), custom_call_target="tpu_custom_call" | custom-call | tf_op jit(solution)/shard_map/pallas_call | solution.py:367
  49.6 7.6 %all-to-all-start.1 = ((bf16[64,16,128]{2,1,0:T(8,128)(2,1)}), bf16[64,16,128]{2,1,0:T(8,128)(2,1)S(1)}, u32[]{:S(2)}, u32[]{:S(2)}) async-start(bf16[64,16,128]{2,1,0:T(8,128)(2,1)} %get-tuple-element.25), calls=%async_computation.1 | async-start | bytes 524288 | tf_op jit(solution)/shard_map/all_to_all | solution.py:385
  57.2 2.5 %collective-permute-start = (bf16[1344,128]{1,0:T(8,128)(2,1)S(1)}, bf16[1344,128]{1,0:T(8,128)(2,1)S(1)}, u32[]{:S(2)}, u32[]{:S(2)}) collective-permute-start(bf16[1344,128]{1,0:T(8,128)(2,1)S(1)} %get-tuple-element.27), channel_id=1, source_target_pairs={{0,1},{1,0},{2,3},{3,2},{4,5},{5,4},{6,7},{7,6},{8,9},{9,8},{10,11... | collective-permute-start | bytes 1032200 | tf_op jit(solution)/shard_map/ppermute | solution.py:389
  59.8 0.1 copy.28
  59.9 0.1 copy.27
  60.0 0.8 collective-permute-done.end_got_ref
  60.9 10.2 %all-to-all-done.1.recv_ref = bf16[64,16,128]{2,1,0:T(8,128)(2,1)S(1)} async-done(((bf16[64,16,128]{2,1,0:T(8,128)(2,1)}), bf16[64,16,128]{2,1,0:T(8,128)(2,1)S(1)}, u32[]{:S(2)}, u32[]{:S(2)}) %all-to-all-start.1) | async-done | bytes 262176 | tf_op jit(solution)/shard_map/all_to_all | solution.py:385
  71.1 6.9 %shard_map.155 = (bf16[4,256,128]{2,1,0:T(8,128)(2,1)}, bf16[64,32,128]{2,1,0:T(8,128)(2,1)}, bf16[1024,128]{1,0:T(8,128)(2,1)S(1)}, f32[1024,128]{1,0:T(8,128)S(1)}) custom-call(bf16[4,256,128]{2,1,0:T(8,128)(2,1)S(1)} %copy-done.1, bf16[64,16,128]{2,1,0:T(8,128)(2,1)S(1)} %all-to-all-done.1.recv_ref, bf16[4,256,256]{2,1,0:T(8,128)(2,1)S(1)} %bitcast.8, ...), custom_call_target="tpu_custom_call" | custom-call | tf_op jit(solution)/shard_map/pallas_call | solution.py:367
  77.9 6.2 %all-to-all-start.2 = ((bf16[64,32,128]{2,1,0:T(8,128)(2,1)}), bf16[64,32,128]{2,1,0:T(8,128)(2,1)S(1)}, u32[]{:S(2)}, u32[]{:S(2)}) async-start(bf16[64,32,128]{2,1,0:T(8,128)(2,1)} %get-tuple-element.29), calls=%async_computation.2 | async-start | bytes 1048576 | tf_op jit(solution)/shard_map/all_to_all | solution.py:385
  84.2 2.4 %collective-permute-start.1 = (bf16[1024,128]{1,0:T(8,128)(2,1)S(1)}, bf16[1024,128]{1,0:T(8,128)(2,1)S(1)}, u32[]{:S(2)}, u32[]{:S(2)}) collective-permute-start(bf16[1024,128]{1,0:T(8,128)(2,1)S(1)} %get-tuple-element.31), channel_id=1, source_target_pairs={{0,1},{1,0},{2,3},{3,2},{4,5},{5,4},{6,7},{7,6},{8,9},{9,8},{10,11... | collective-permute-start | bytes 786440 | tf_op jit(solution)/shard_map/ppermute | solution.py:389
  86.5 1.1 collective-permute-done.1.got_ref
  87.7 15.1 %all-to-all-done.2.recv_ref = bf16[64,32,128]{2,1,0:T(8,128)(2,1)S(1)} async-done(((bf16[64,32,128]{2,1,0:T(8,128)(2,1)}), bf16[64,32,128]{2,1,0:T(8,128)(2,1)S(1)}, u32[]{:S(2)}, u32[]{:S(2)}) %all-to-all-start.2) | async-done | bytes 524320 | tf_op jit(solution)/shard_map/all_to_all | solution.py:385
  102.8 0.7 shard_map.156
  103.5 20.6 %all_to_all.24.recv_ref = bf16[32,56,128]{2,1,0:T(8,128)(2,1)S(1)} all-to-all(bf16[32,56,128]{2,1,0:T(8,128)(2,1)S(1)} %get-tuple-element.32), channel_id=1, replica_groups=mesh['dp'=8,'chip'=32,'core'=2] {'chip'}, dimensions={0} | all-to-all | bytes 917504 | tf_op jit(solution)/shard_map/all_to_all | solution.py:385
  124.1 5.8 %all_gather.3.totals_ref = bf16[64,24,128]{2,1,0:T(8,128)(2,1)S(1)} all-gather(bf16[32,24,128]{2,1,0:T(8,128)(2,1)S(1)} %shard_map.157), channel_id=1, replica_groups=mesh['dp'=8,'chip'=32,'core'=2] {'core'}, dimensions={0}, use_global_device_ids=true | all-gather | bytes 589824 | tf_op jit(solution)/shard_map/all_gather | solution.py:449
  129.9 1.0 shard_map.158
  (16 shorter events, 0.1 us)
Async XLA Ops:
  1.3 1.4 %copy-start = (bf16[128,512]{1,0:T(8,128)(2,1)S(1)}, bf16[128,512]{1,0:T(8,128)(2,1)}, u32[]{:S(2)}) copy-start(bf16[128,512]{1,0:T(8,128)(2,1)} %w_in_ref.5) | copy-start | bytes 393220
  1.3 1.4 %copy-start.1 = (bf16[4,256,128]{2,1,0:T(8,128)(2,1)S(1)}, bf16[4,256,128]{2,1,0:T(8,128)(2,1)}, u32[]{:S(2)}) copy-start(bf16[4,256,128]{2,1,0:T(8,128)(2,1)} %x_ref.3) | copy-start | bytes 786436
  1.3 1.4 %copy-start.3 = (bf16[4,256,128]{2,1,0:T(8,128)(2,1)S(1)}, bf16[4,256,128]{2,1,0:T(8,128)(2,1)}, u32[]{:S(2)}) copy-start(bf16[4,256,128]{2,1,0:T(8,128)(2,1)} %cot_ref.1) | copy-start | bytes 786436
  1.3 1.4 %copy-start.4 = (bf16[128,128]{1,0:T(8,128)(2,1)S(1)}, bf16[128,128]{1,0:T(8,128)(2,1)}, u32[]{:S(2)}) copy-start(bf16[128,128]{1,0:T(8,128)(2,1)} %w_out_ref.1) | copy-start | bytes 98308
  1.3 1.4 %copy-start.5 = (s32[4096]{0:T(1024)S(1)}, s32[4096]{0:T(1024)}, u32[]{:S(2)}) copy-start(s32[4096]{0:T(1024)} %param.18) | copy-start | bytes 49156
  6.6 17.8 %copy-start.7 = (bf16[128,128]{1,0:T(8,128)(2,1)S(1)}, bf16[128,128]{1,0:T(8,128)(2,1)}, u32[]{:S(2)}) copy-start(bf16[128,128]{1,0:T(8,128)(2,1)} %param.17) | copy-start | bytes 98308
  6.6 17.9 %copy-start.2 = (bf16[128,512]{1,0:T(8,128)(2,1)S(1)}, bf16[128,512]{1,0:T(8,128)(2,1)}, u32[]{:S(2)}) copy-start(bf16[128,512]{1,0:T(8,128)(2,1)} %w_in_ref.4) | copy-start | bytes 393220
  6.6 18.0 %copy-start.6 = (bf16[256,4,256]{2,1,0:T(4,128)(2,1)S(1)}, bf16[256,4,256]{2,1,0:T(4,128)(2,1)}, u32[]{:S(2)}) copy-start(bf16[256,4,256]{2,1,0:T(4,128)(2,1)} %param.13) | copy-start | bytes 1572868
  6.6 36.5 %all-to-all-start = ((bf16[64,32,128]{2,1,0:T(8,128)(2,1)}), bf16[64,32,128]{2,1,0:T(8,128)(2,1)S(1)}, u32[]{:S(2)}, u32[]{:S(2)}) async-start(bf16[64,32,128]{2,1,0:T(8,128)(2,1)} %get-tuple-element.23), calls=%async_computation | async-start | bytes 1048576 | tf_op jit(solution)/shard_map/all_to_all | solution.py:385
  49.6 21.5 %all-to-all-start.1 = ((bf16[64,16,128]{2,1,0:T(8,128)(2,1)}), bf16[64,16,128]{2,1,0:T(8,128)(2,1)S(1)}, u32[]{:S(2)}, u32[]{:S(2)}) async-start(bf16[64,16,128]{2,1,0:T(8,128)(2,1)} %get-tuple-element.25), calls=%async_computation.1 | async-start | bytes 524288 | tf_op jit(solution)/shard_map/all_to_all | solution.py:385
  57.2 3.6 %collective-permute-start = (bf16[1344,128]{1,0:T(8,128)(2,1)S(1)}, bf16[1344,128]{1,0:T(8,128)(2,1)S(1)}, u32[]{:S(2)}, u32[]{:S(2)}) collective-permute-start(bf16[1344,128]{1,0:T(8,128)(2,1)S(1)} %get-tuple-element.27), channel_id=1, source_target_pairs={{0,1},{1,0},{2,3},{3,2},{4,5},{5,4},{6,7},{7,6},{8,9},{9,8},{10,11... | collective-permute-start | bytes 1032200 | tf_op jit(solution)/shard_map/ppermute | solution.py:389
  77.9 24.8 %all-to-all-start.2 = ((bf16[64,32,128]{2,1,0:T(8,128)(2,1)}), bf16[64,32,128]{2,1,0:T(8,128)(2,1)S(1)}, u32[]{:S(2)}, u32[]{:S(2)}) async-start(bf16[64,32,128]{2,1,0:T(8,128)(2,1)} %get-tuple-element.29), calls=%async_computation.2 | async-start | bytes 1048576 | tf_op jit(solution)/shard_map/all_to_all | solution.py:385
  84.2 3.5 %collective-permute-start.1 = (bf16[1024,128]{1,0:T(8,128)(2,1)S(1)}, bf16[1024,128]{1,0:T(8,128)(2,1)S(1)}, u32[]{:S(2)}, u32[]{:S(2)}) collective-permute-start(bf16[1024,128]{1,0:T(8,128)(2,1)S(1)} %get-tuple-element.31), channel_id=1, source_target_pairs={{0,1},{1,0},{2,3},{3,2},{4,5},{5,4},{6,7},{7,6},{8,9},{9,8},{10,11... | collective-permute-start | bytes 786440 | tf_op jit(solution)/shard_map/ppermute | solution.py:389

commit v5 on v4

--- a/solution.py
+++ b/solution.py
@@ -114,6 +114,23 @@
 
 def wide_penalty(penalty):
     return jnp.concatenate([penalty] * (N // C), axis=1)
+
+
+TILE = 8
+
+
+def spread(rows, ref):
+    for i in range(rows.shape[1] // TILE):
+        ref[:, :, i * C : (i + 1) * C] = rows[:, i * TILE : (i + 1) * TILE].astype(bf16)
+
+
+def collect(ref, first, last):
+    blocks = [ref[:, :, i * C : (i + 1) * C].astype(f32) for i in range(first // TILE, last // TILE)]
+    return jnp.concatenate(blocks, axis=1)
+
+
+def lanes(peers, rows):
+    return struct((peers, TILE, rows // TILE * C), bf16)
 
 
 def start_forward_kernel(
@@ -139,8 +156,8 @@
     for r in range(R):
         pack_rows(out[r * N : (r + 1) * N], r, stage.at[r], first_packed)
         pack_rows(cot_ref[r].astype(f32), r, stage.at[R + r], cot_packed)
-    send_ref[:, : R * R, :] = first_packed[...].reshape(PEERS, R * R, C).astype(bf16)
-    send_ref[:, R * R :, :] = cot_packed[...].reshape(PEERS, R * R, C).astype(bf16)
+    both = [part[...].reshape(PEERS, R * R, C) for part in (first_packed, cot_packed)]
+    spread(jnp.concatenate(both, axis=1), send_ref)
 
 
 def node_states(x, bias_ref, penalty, w_in_ref, masks):
@@ -259,8 +276,8 @@
     masks = head_masks()
     core = core_index()
     penalty = wide_penalty(pen_ref[...])
-    x_all[...] = recv_ref[:, : R * R, :].astype(f32).reshape(N * R, C)
-    up_all[...] = recv_ref[:, R * R :, :].astype(f32).reshape(N * R, C)
+    x_all[...] = collect(recv_ref, 0, R * R).reshape(N * R, C)
+    up_all[...] = collect(recv_ref, R * R, 2 * R * R).reshape(N * R, C)
     for first in range(0, R, GROUP):
         group = range(first, first + GROUP)
         x = jnp.concatenate([x_all[pl.ds(r, N, stride=R), :] for r in group], axis=0)
@@ -269,7 +286,7 @@
         grads = node_backward(first == 0, states, upstreams, w_in_t_ref, w_out_t_ref, masks, bias_sum, weight_sum)
         for r, grad in zip(group, grads):
             pack_rows(grad, r, stage.at[r], grad_packed)
-    send_ref[...] = grad_packed[...].reshape(PEERS, R * R, C).astype(bf16)
+    spread(grad_packed[...].reshape(PEERS, R * R, C), send_ref)
     terms = bias_terms(bias_sum, bias_packed)
     for parity in range(2):
         even, odd = (terms[:, 2 * parity + i].reshape(PEERS * CHUNKS, C) for i in range(2))
@@ -287,7 +304,7 @@
     masks = head_masks()
     core = core_index()
     penalty = wide_penalty(pen_ref[...])
-    up_all[...] = recv_ref[...].astype(f32).reshape(N * R, C)
+    up_all[...] = collect(recv_ref, 0, R * R).reshape(N * R, C)
     for first in range(0, R, GROUP):
         group = range(first, first + GROUP)
         x = x_ref[first : first + GROUP].reshape(GROUP * N, C).astype(f32)
@@ -306,7 +323,7 @@
         weight_packed[pl.ds(2 * WEIGHT_BLOCKS + q, PEERS, stride=WEIGHT_ROWS), :] = block
     end_bias = by_parity(end_terms[:BIAS_HALF])
     weights = weight_packed[...].reshape(PEERS, WEIGHT_ROWS, C)
-    send_ref[...] = jnp.concatenate(end_bias + [weights], axis=1).astype(bf16)
+    spread(jnp.concatenate(end_bias + [weights], axis=1), send_ref)
     terms = bias_terms(bias_sum, bias_packed).reshape(CHIPS, 2, R * CHUNKS, C)
     even, odd = (terms[:, i].reshape(BIAS_HALF, C) for i in range(2))
     core_split(even, odd, core, keep_ref, give_ref, slice(None))
@@ -324,7 +341,7 @@
 
 
 def middle_kernel(recv_ref, keep_ref, got_ref, send_ref, bias_ref):
-    by_core = jnp.sum(recv_ref[...].astype(f32).reshape(CHIPS, 2, TERM_ROWS, C), axis=0)
+    by_core = jnp.sum(collect(recv_ref, 0, TERM_ROWS).reshape(CHIPS, 2, TERM_ROWS, C), axis=0)
     for parity in range(2):
         for core in range(2):
             write_bias(by_core[core, parity * CHUNKS : (parity + 1) * CHUNKS], 2 * parity + core, bias_ref)
@@ -333,15 +350,15 @@
     totals = jnp.concatenate([even + jnp.where(slot < 2 * WEIGHT_BLOCKS, odd, 0.0), odd[CHUNKS:]], axis=0)
     bias_rows = (keep_ref[...] + got_ref[...].astype(f32)).reshape(CHIPS, R * CHUNKS, C)
     everyone = jnp.broadcast_to(totals[None], (CHIPS, TOTAL_ROWS, C))
-    send_ref[...] = jnp.concatenate([bias_rows, everyone], axis=1).astype(bf16)
+    spread(jnp.concatenate([bias_rows, everyone], axis=1), send_ref)
 
 
 def totals_kernel(recv_ref, totals_ref):
-    totals_ref[...] = recv_ref[...].astype(f32)[:, R * CHUNKS :].astype(bf16)
+    totals_ref[...] = collect(recv_ref, R * CHUNKS, R * CHUNKS + TOTAL_ROWS).astype(bf16)
 
 
 def last_kernel(recv_ref, totals_ref, bias_ref, in_start, out_start, in_end, out_end, stage, block):
-    bias = jnp.sum(recv_ref[...].astype(f32)[:, : R * CHUNKS], axis=0)
+    bias = jnp.sum(collect(recv_ref, 0, R * CHUNKS), axis=0)
     for residue in range(R):
         write_bias(bias[residue * CHUNKS : (residue + 1) * CHUNKS], residue, bias_ref)
     stage[...] = totals_ref[...].astype(f32).reshape(PEERS * TOTAL_ROWS, C) * (1.0 / N)
@@ -381,8 +398,7 @@
 
 
 def exchange(value, axes=("chip", "core")):
-    rows = value.reshape(-1, C)
-    return lax.all_to_all(rows, axes, split_axis=0, concat_axis=0, tiled=True).reshape(value.shape)
+    return lax.all_to_all(value, axes, split_axis=0, concat_axis=0, tiled=True)
 
 
 def swap(value):
@@ -412,7 +428,7 @@
 
     send, penalty = call(
         start_forward_kernel,
-        (struct((PEERS, 2 * R * R, C), bf16), struct((N, C), f32)),
+        (lanes(PEERS, 2 * R * R), struct((N, C), f32)),
         (pltpu.VMEM((2 * R, N, C), f32), rows_f32, rows_f32),
         {4: pltpu.SMEM},
     )(pair_act, cotangent, bias_start_t, residue_mask.reshape(CHAIN // C, C), window_offset, w_in_start, w_out_start)
@@ -420,7 +436,7 @@
     grad_send, end_give, end_keep = call(
         end_kernel,
         (
-            struct((PEERS, R * R, C), bf16),
+            lanes(PEERS, R * R),
             struct((BIAS_HALF + WEIGHT_HALF, C), bf16),
             struct((BIAS_HALF + WEIGHT_HALF, C), f32),
         ),
@@ -432,7 +448,7 @@
         start_kernel,
         (
             struct((R, N, C), bf16),
-            struct((PEERS, TERM_ROWS, C), bf16),
+            lanes(PEERS, TERM_ROWS),
             struct((BIAS_HALF, C), bf16),
             struct((BIAS_HALF, C), f32),
         ),
@@ -442,7 +458,7 @@
     start_got = swap(start_give)
     last_rows = R * CHUNKS + TOTAL_ROWS
     last_send, grad_bias_end = call(
-        middle_kernel, (struct((CHIPS, last_rows, C), bf16), struct((R, H, N), f32))
+        middle_kernel, (lanes(CHIPS, last_rows), struct((R, H, N), f32))
     )(term_recv, start_keep, start_got)
     last_recv = exchange(last_send, "chip")
     totals = call(totals_kernel, struct((CHIPS, TOTAL_ROWS, C), bf16))(last_recv)

time: 131 us -> 132 us (level)
  no operation moved by 1% of the time
where the time goes in v5:
time: 132 us; the launch traced here: 131 us
  waiting for transfers between devices  45.4 us (34%)
  starting transfers between devices  36.5 us (28%)
  blocking collectives  26.4 us (20%)
  Pallas kernels  18.9 us (14%)
  local copies, waits for them, and re-layouts  2.21 us (2%)
  between operations  1.47 us (1%)
    all_to_all x3, waiting for transfers between devices, exchange(): return lax.all_to_all(value, axes, split_axis=0, concat_axis=0, tiled=True)  43.5 us
    all_to_all x3, starting transfers between devices, exchange(): return lax.all_to_all(value, axes, split_axis=0, concat_axis=0, tiled=True)  31.6 us
    all_to_all x1, blocking collectives, exchange(): return lax.all_to_all(value, axes, split_axis=0, concat_axis=0, tiled=True)  20.6 us
    pallas_call x6, Pallas kernels, apply(): pl.pallas_call(kernel, out_shape=outs, in_specs=[pl.BlockSpec(memory_spac...  18.9 us
    all_gather x1, blocking collectives, shards(): totals = lax.all_gather(totals, 'core', axis=0, tiled=True)  5.82 us
    ppermute x2, starting transfers between devices, swap(): return lax.ppermute(value, 'core', [(0, 1), (1, 0)])  4.91 us
  transfers between devices with their start and end apart: 5, of which 5 were waited for; matrix products, arithmetic and copies ran while one was open for 1% of the time, Pallas kernels for 0%

profile of v5, /device:TPU:1, one launch (start us, length us, event | category | flops | bytes accessed | tf_op | source)
XLA Modules:
  0.0 130.9 jit_solution(8783587457086990520)
XLA Ops:
  1.3 1.4 %copy.23 = bf16[256,4,256]{0,2,1:T(8,128)(2,1)S(1)} copy(bf16[256,4,256]{2,1,0:T(4,128)(2,1)} %param.12) | data formatting | bytes 1048576 | tf_op args[2]
  2.7 0.0 copy-done
  2.8 3.8 %shard_map.153 = (bf16[64,8,512]{2,1,0:T(8,128)(2,1)}, f32[256,128]{1,0:T(8,128)S(1)}) custom-call(bf16[4,256,128]{2,1,0:T(8,128)(2,1)S(1)} %copy-done.1, bf16[4,256,128]{2,1,0:T(8,128)(2,1)S(1)} %copy-done.3, bf16[4,256,256]{2,1,0:T(8,128)(2,1)S(1)} %bitcast.7, s32[32,128]{1,0:T(8,128)S(1)} %bitcast.14, s32[1]{0:T(128)S(6)} %copy.29.offset_ref, ...), custom_call_target="tpu_custom_call" | custom-call | tf_op jit(solution)/shard_map/pallas_call | solution.py:384
  6.6 17.8 %all-to-all-start = ((bf16[64,8,512]{2,1,0:T(8,128)(2,1)}), bf16[64,8,512]{2,1,0:T(8,128)(2,1)S(1)}, u32[]{:S(2)}, u32[]{:S(2)}) async-start(bf16[64,8,512]{2,1,0:T(8,128)(2,1)} %get-tuple-element.23), calls=%async_computation | async-start | bytes 1048576 | tf_op jit(solution)/shard_map/all_to_all | solution.py:401
  24.4 0.1 copy.26
  24.5 0.1 copy.25
  24.7 0.3 copy.24
  25.0 18.1 %all-to-all-done.recv_ref = bf16[64,8,512]{2,1,0:T(8,128)(2,1)S(1)} async-done(((bf16[64,8,512]{2,1,0:T(8,128)(2,1)}), bf16[64,8,512]{2,1,0:T(8,128)(2,1)S(1)}, u32[]{:S(2)}, u32[]{:S(2)}) %all-to-all-start) | async-done | bytes 524320 | tf_op jit(solution)/shard_map/all_to_all | solution.py:401
  43.1 6.5 %shard_map.154 = (bf16[64,8,256]{2,1,0:T(8,128)(2,1)}, bf16[1344,128]{1,0:T(8,128)(2,1)S(1)}, f32[1344,128]{1,0:T(8,128)S(1)}) custom-call(bf16[64,8,512]{2,1,0:T(8,128)(2,1)S(1)} %all-to-all-done.recv_ref, bf16[4,256,256]{2,1,0:T(8,128)(2,1)S(1)} %bitcast.9, f32[256,128]{1,0:T(8,128)S(1)} %get-tuple-element.24.pen_ref, bf16[128,512]{1,0:T(8,128)(2,1)S(1)} %copy-done.2, ...), custom_call_target="tpu_custom_call" | custom-call | tf_op jit(solution)/shard_map/pallas_call | solution.py:384
  49.6 7.6 %all-to-all-start.1 = ((bf16[64,8,256]{2,1,0:T(8,128)(2,1)}), bf16[64,8,256]{2,1,0:T(8,128)(2,1)S(1)}, u32[]{:S(2)}, u32[]{:S(2)}) async-start(bf16[64,8,256]{2,1,0:T(8,128)(2,1)} %get-tuple-element.25), calls=%async_computation.1 | async-start | bytes 524288 | tf_op jit(solution)/shard_map/all_to_all | solution.py:401
  57.3 2.5 %collective-permute-start = (bf16[1344,128]{1,0:T(8,128)(2,1)S(1)}, bf16[1344,128]{1,0:T(8,128)(2,1)S(1)}, u32[]{:S(2)}, u32[]{:S(2)}) collective-permute-start(bf16[1344,128]{1,0:T(8,128)(2,1)S(1)} %get-tuple-element.27), channel_id=1, source_target_pairs={{0,1},{1,0},{2,3},{3,2},{4,5},{5,4},{6,7},{7,6},{8,9},{9,8},{10,11... | collective-permute-start | bytes 1032200 | tf_op jit(solution)/shard_map/ppermute | solution.py:405
  59.8 0.1 copy.28
  59.9 0.1 copy.27
  60.1 0.8 collective-permute-done.end_got_ref
  60.9 10.2 %all-to-all-done.1.recv_ref = bf16[64,8,256]{2,1,0:T(8,128)(2,1)S(1)} async-done(((bf16[64,8,256]{2,1,0:T(8,128)(2,1)}), bf16[64,8,256]{2,1,0:T(8,128)(2,1)S(1)}, u32[]{:S(2)}, u32[]{:S(2)}) %all-to-all-start.1) | async-done | bytes 262176 | tf_op jit(solution)/shard_map/all_to_all | solution.py:401
  71.1 6.9 %shard_map.155 = (bf16[4,256,128]{2,1,0:T(8,128)(2,1)}, bf16[64,8,512]{2,1,0:T(8,128)(2,1)}, bf16[1024,128]{1,0:T(8,128)(2,1)S(1)}, f32[1024,128]{1,0:T(8,128)S(1)}) custom-call(bf16[4,256,128]{2,1,0:T(8,128)(2,1)S(1)} %copy-done.1, bf16[64,8,256]{2,1,0:T(8,128)(2,1)S(1)} %all-to-all-done.1.recv_ref, bf16[4,256,256]{2,1,0:T(8,128)(2,1)S(1)} %bitcast.8, ...), custom_call_target="tpu_custom_call" | custom-call | tf_op jit(solution)/shard_map/pallas_call | solution.py:384
  78.0 6.2 %all-to-all-start.2 = ((bf16[64,8,512]{2,1,0:T(8,128)(2,1)}), bf16[64,8,512]{2,1,0:T(8,128)(2,1)S(1)}, u32[]{:S(2)}, u32[]{:S(2)}) async-start(bf16[64,8,512]{2,1,0:T(8,128)(2,1)} %get-tuple-element.29), calls=%async_computation.2 | async-start | bytes 1048576 | tf_op jit(solution)/shard_map/all_to_all | solution.py:401
  84.2 2.4 %collective-permute-start.1 = (bf16[1024,128]{1,0:T(8,128)(2,1)S(1)}, bf16[1024,128]{1,0:T(8,128)(2,1)S(1)}, u32[]{:S(2)}, u32[]{:S(2)}) collective-permute-start(bf16[1024,128]{1,0:T(8,128)(2,1)S(1)} %get-tuple-element.31), channel_id=1, source_target_pairs={{0,1},{1,0},{2,3},{3,2},{4,5},{5,4},{6,7},{7,6},{8,9},{9,8},{10,11... | collective-permute-start | bytes 786440 | tf_op jit(solution)/shard_map/ppermute | solution.py:405
  86.6 1.1 collective-permute-done.1.got_ref
  87.7 15.1 %all-to-all-done.2.recv_ref = bf16[64,8,512]{2,1,0:T(8,128)(2,1)S(1)} async-done(((bf16[64,8,512]{2,1,0:T(8,128)(2,1)}), bf16[64,8,512]{2,1,0:T(8,128)(2,1)S(1)}, u32[]{:S(2)}, u32[]{:S(2)}) %all-to-all-start.2) | async-done | bytes 524320 | tf_op jit(solution)/shard_map/all_to_all | solution.py:401
  102.8 0.7 shard_map.156
  103.5 20.6 %all_to_all.20.recv_ref = bf16[32,8,896]{2,1,0:T(8,128)(2,1)S(1)} all-to-all(bf16[32,8,896]{2,1,0:T(8,128)(2,1)S(1)} %get-tuple-element.32), channel_id=1, replica_groups=mesh['dp'=8,'chip'=32,'core'=2] {'chip'}, dimensions={0} | all-to-all | bytes 917504 | tf_op jit(solution)/shard_map/all_to_all | solution.py:401
  124.1 5.8 %all_gather.3.totals_ref = bf16[64,24,128]{2,1,0:T(8,128)(2,1)S(1)} all-gather(bf16[32,24,128]{2,1,0:T(8,128)(2,1)S(1)} %shard_map.157), channel_id=1, replica_groups=mesh['dp'=8,'chip'=32,'core'=2] {'core'}, dimensions={0}, use_global_device_ids=true | all-gather | bytes 589824 | tf_op jit(solution)/shard_map/all_gather | solution.py:465
  130.0 1.0 shard_map.158
  (16 shorter events, 0.1 us)
Async XLA Ops:
  1.3 1.4 %copy-start = (bf16[128,512]{1,0:T(8,128)(2,1)S(1)}, bf16[128,512]{1,0:T(8,128)(2,1)}, u32[]{:S(2)}) copy-start(bf16[128,512]{1,0:T(8,128)(2,1)} %w_in_ref.5) | copy-start | bytes 393220
  1.3 1.4 %copy-start.1 = (bf16[4,256,128]{2,1,0:T(8,128)(2,1)S(1)}, bf16[4,256,128]{2,1,0:T(8,128)(2,1)}, u32[]{:S(2)}) copy-start(bf16[4,256,128]{2,1,0:T(8,128)(2,1)} %x_ref.3) | copy-start | bytes 786436
  1.3 1.4 %copy-start.3 = (bf16[4,256,128]{2,1,0:T(8,128)(2,1)S(1)}, bf16[4,256,128]{2,1,0:T(8,128)(2,1)}, u32[]{:S(2)}) copy-start(bf16[4,256,128]{2,1,0:T(8,128)(2,1)} %cot_ref.1) | copy-start | bytes 786436
  1.3 1.4 %copy-start.4 = (bf16[128,128]{1,0:T(8,128)(2,1)S(1)}, bf16[128,128]{1,0:T(8,128)(2,1)}, u32[]{:S(2)}) copy-start(bf16[128,128]{1,0:T(8,128)(2,1)} %w_out_ref.1) | copy-start | bytes 98308
  1.3 1.4 %copy-start.5 = (s32[4096]{0:T(1024)S(1)}, s32[4096]{0:T(1024)}, u32[]{:S(2)}) copy-start(s32[4096]{0:T(1024)} %param.18) | copy-start | bytes 49156
  6.6 17.8 %copy-start.7 = (bf16[128,128]{1,0:T(8,128)(2,1)S(1)}, bf16[128,128]{1,0:T(8,128)(2,1)}, u32[]{:S(2)}) copy-start(bf16[128,128]{1,0:T(8,128)(2,1)} %param.17) | copy-start | bytes 98308
  6.6 17.9 %copy-start.2 = (bf16[128,512]{1,0:T(8,128)(2,1)S(1)}, bf16[128,512]{1,0:T(8,128)(2,1)}, u32[]{:S(2)}) copy-start(bf16[128,512]{1,0:T(8,128)(2,1)} %w_in_ref.4) | copy-start | bytes 393220
  6.6 18.0 %copy-start.6 = (bf16[256,4,256]{2,1,0:T(4,128)(2,1)S(1)}, bf16[256,4,256]{2,1,0:T(4,128)(2,1)}, u32[]{:S(2)}) copy-start(bf16[256,4,256]{2,1,0:T(4,128)(2,1)} %param.13) | copy-start | bytes 1572868
  6.6 36.5 %all-to-all-start = ((bf16[64,8,512]{2,1,0:T(8,128)(2,1)}), bf16[64,8,512]{2,1,0:T(8,128)(2,1)S(1)}, u32[]{:S(2)}, u32[]{:S(2)}) async-start(bf16[64,8,512]{2,1,0:T(8,128)(2,1)} %get-tuple-element.23), calls=%async_computation | async-start | bytes 1048576 | tf_op jit(solution)/shard_map/all_to_all | solution.py:401
  49.6 21.5 %all-to-all-start.1 = ((bf16[64,8,256]{2,1,0:T(8,128)(2,1)}), bf16[64,8,256]{2,1,0:T(8,128)(2,1)S(1)}, u32[]{:S(2)}, u32[]{:S(2)}) async-start(bf16[64,8,256]{2,1,0:T(8,128)(2,1)} %get-tuple-element.25), calls=%async_computation.1 | async-start | bytes 524288 | tf_op jit(solution)/shard_map/all_to_all | solution.py:401
  57.3 3.6 %collective-permute-start = (bf16[1344,128]{1,0:T(8,128)(2,1)S(1)}, bf16[1344,128]{1,0:T(8,128)(2,1)S(1)}, u32[]{:S(2)}, u32[]{:S(2)}) collective-permute-start(bf16[1344,128]{1,0:T(8,128)(2,1)S(1)} %get-tuple-element.27), channel_id=1, source_target_pairs={{0,1},{1,0},{2,3},{3,2},{4,5},{5,4},{6,7},{7,6},{8,9},{9,8},{10,11... | collective-permute-start | bytes 1032200 | tf_op jit(solution)/shard_map/ppermute | solution.py:405
  78.0 24.8 %all-to-all-start.2 = ((bf16[64,8,512]{2,1,0:T(8,128)(2,1)}), bf16[64,8,512]{2,1,0:T(8,128)(2,1)S(1)}, u32[]{:S(2)}, u32[]{:S(2)}) async-start(bf16[64,8,512]{2,1,0:T(8,128)(2,1)} %get-tuple-element.29), calls=%async_computation.2 | async-start | bytes 1048576 | tf_op jit(solution)/shard_map/all_to_all | solution.py:401
  84.2 3.5 %collective-permute-start.1 = (bf16[1024,128]{1,0:T(8,128)(2,1)S(1)}, bf16[1024,128]{1,0:T(8,128)(2,1)S(1)}, u32[]{:S(2)}, u32[]{:S(2)}) collective-permute-start(bf16[1024,128]{1,0:T(8,128)(2,1)S(1)} %get-tuple-element.31), channel_id=1, source_target_pairs={{0,1},{1,0},{2,3},{3,2},{4,5},{5,4},{6,7},{7,6},{8,9},{9,8},{10,11... | collective-permute-start | bytes 786440 | tf_op jit(solution)/shard_map/ppermute | solution.py:405
